TPU v7x, 32 devices: a whole 2x2x4 slice. The times are simulated.
32 devices in a mesh: dp: 8 (over z, y), fsdp: 4 (over x, core).
Axes of the slice: x: 2, y: 2, z: 4, core: 2. Of those that a mesh axis runs over, the one named last changes fastest.
Arguments:
- tokens: bfloat16 [8, 4, 1528, 384], P('dp', 'fsdp'), may hold values from -6 to 6
- focal_count: int32 [8, 4], P('dp', 'fsdp'), may hold values from 0 to 20
- cls_order: int32 [4, 192], P('fsdp', 'dp'), may hold values from 0 to 191, each once within a row
- out_cotangent: bfloat16 [8, 4, 1528, 384], P('dp', 'fsdp'), may hold values from -6 to 6
- cls_cotangent: bfloat16 [8, 4, 24, 384], P('dp', 'fsdp'), may hold values from -6 to 6
- qkv_weight: float32 [2, 384, 1152], P(None, 'dp', 'fsdp'), may hold values from -0.3125 to 0.3125
- proj_weight: float32 [2, 384, 384], P(None, 'dp', 'fsdp'), may hold values from -0.625 to 0.625
- fc1_weight: float32 [2, 384, 1536], P(None, 'dp', 'fsdp'), may hold values from -0.3125 to 0.3125
- fc2_weight: float32 [2, 1536, 384], P(None, 'dp', 'fsdp'), may hold values from -0.15625 to 0.15625
- vec_params: float32 [2, 384, 12], P(None, 'dp', 'fsdp'), may hold values from -1.2 to 1.5, as said below
- qkv_first: float32 [2, 384, 1152], P(None, 'dp', 'fsdp'), may hold values from -640 to 640
- proj_first: float32 [2, 384, 384], P(None, 'dp', 'fsdp'), may hold values from -640 to 640
- fc1_first: float32 [2, 384, 1536], P(None, 'dp', 'fsdp'), may hold values from -640 to 640
- fc2_first: float32 [2, 1536, 384], P(None, 'dp', 'fsdp'), may hold values from -640 to 640
- vec_first: float32 [2, 384, 12], P(None, 'dp', 'fsdp'), may hold values from -640 to 640
- qkv_second: float32 [2, 384, 1152], P(None, 'dp', 'fsdp'), may hold values from 12224 to 48896
- proj_second: float32 [2, 384, 384], P(None, 'dp', 'fsdp'), may hold values from 12224 to 48896
- fc1_second: float32 [2, 384, 1536], P(None, 'dp', 'fsdp'), may hold values from 12224 to 48896
- fc2_second: float32 [2, 1536, 384], P(None, 'dp', 'fsdp'), may hold values from 12224 to 48896
- vec_second: float32 [2, 384, 12], P(None, 'dp', 'fsdp'), may hold values from 12224 to 48896
Outputs:
- activations: bfloat16 [8, 4, 1528, 384], P('dp', 'fsdp')
- cls_regrouped: bfloat16 [8, 4, 24, 384], P('dp', 'fsdp')
- input_grad: float32 [8, 4, 1528, 384], P('dp', 'fsdp')
- qkv_new: float32 [2, 384, 1152], P(None, 'dp', 'fsdp')
- proj_new: float32 [2, 384, 384], P(None, 'dp', 'fsdp')
- fc1_new: float32 [2, 384, 1536], P(None, 'dp', 'fsdp')
- fc2_new: float32 [2, 1536, 384], P(None, 'dp', 'fsdp')
- vec_new: float32 [2, 384, 12], P(None, 'dp', 'fsdp')
- qkv_first_new: float32 [2, 384, 1152], P(None, 'dp', 'fsdp')
- proj_first_new: float32 [2, 384, 384], P(None, 'dp', 'fsdp')
- fc1_first_new: float32 [2, 384, 1536], P(None, 'dp', 'fsdp')
- fc2_first_new: float32 [2, 1536, 384], P(None, 'dp', 'fsdp')
- vec_first_new: float32 [2, 384, 12], P(None, 'dp', 'fsdp')
- qkv_second_new: float32 [2, 384, 1152], P(None, 'dp', 'fsdp')
- proj_second_new: float32 [2, 384, 384], P(None, 'dp', 'fsdp')
- fc1_second_new: float32 [2, 384, 1536], P(None, 'dp', 'fsdp')
- fc2_second_new: float32 [2, 1536, 384], P(None, 'dp', 'fsdp')
- vec_second_new: float32 [2, 384, 12], P(None, 'dp', 'fsdp')
Inputs may be any that keep to these rules, and one draw needn't show every extreme that they name: `vec_params`: columns 0 and 2 of each block are gains, the others biases. `cls_order`: each row names every index once.
All inputs are finite; a program needn't handle non-finite values.
Results may differ from a plain program's by a relative error of at most 0.012.
Values may be sent and summed in bfloat16 or wider, within the bound.
A program may use at most 192 MiB of HBM per device.

v0:
```python
from functools import partial

import jax
import jax.numpy as jnp
from jax import lax
from jax.sharding import PartitionSpec as P

HEADS = 6
HEAD_DIM = 64
GLOB_TOK = 197
CROP_TOK = 37
STEP = 5
VIEWS = 4
CROPS = 20


beta_one = 0.5
beta_two = 0.5
step_rate = 0.03
vector_rate = 0.4
weight_decay = 0.05
adam_epsilon = 1e-08
norm_epsilon = 1e-06


def as_sent(value):

    def short(part):
        return part.astype(jnp.bfloat16) if part.dtype == jnp.float32 else part

    return jax.tree.map(short, value)


def layer_norm(inputs, gain_vector, shift_vector):
    centre = jnp.mean(inputs, axis=-1, keepdims=True)
    centred = inputs - centre
    variance = jnp.mean(centred * centred, axis=-1, keepdims=True)
    return centred * lax.rsqrt(variance + norm_epsilon) * gain_vector + shift_vector


def contract_rows(left_side, right_side):
    return lax.dot_general(
        left_side, right_side, (((0,), (0,)), ((), ())), preferred_element_type=jnp.float32
    )


def times_transpose(left_side, right_side):
    return lax.dot_general(
        left_side, right_side, (((1,), (1,)), ((), ())), preferred_element_type=jnp.float32
    )


def over_groups(function, arrays):
    boundary = VIEWS * GLOB_TOK
    glob_parts = [member[:boundary].reshape(VIEWS, GLOB_TOK, HEADS, HEAD_DIM) for member in arrays]
    crop_parts = [member[boundary:].reshape(CROPS, CROP_TOK, HEADS, HEAD_DIM) for member in arrays]
    glob_out = function(*glob_parts)
    crop_out = function(*crop_parts)
    return tuple(
        (
            jnp.concatenate(
                [first_out.reshape(boundary, -1), second_out.reshape(CROPS * CROP_TOK, -1)], axis=0
            )
            for first_out, second_out in zip(glob_out, crop_out)
        )
    )


def attend_forward(queries, key_rows, values):
    score_scale = HEAD_DIM ** (-0.5)
    scores = score_scale * jnp.einsum(
        "bqhe,bkhe->bhqk", queries, key_rows, preferred_element_type=jnp.float32
    )
    soft_probs = jax.nn.softmax(scores, axis=-1).astype(jnp.bfloat16)
    return (jnp.einsum("bhqk,bkhe->bqhe", soft_probs, values, preferred_element_type=jnp.float32),)


def attend_backward(queries, key_rows, values, mixed_grad):
    score_scale = HEAD_DIM ** (-0.5)
    scores = score_scale * jnp.einsum(
        "bqhe,bkhe->bhqk", queries, key_rows, preferred_element_type=jnp.float32
    )
    soft_probs = jax.nn.softmax(scores, axis=-1)
    soft_low = soft_probs.astype(jnp.bfloat16)
    soft_grad = jnp.einsum(
        "bqhe,bkhe->bhqk", mixed_grad, values, preferred_element_type=jnp.float32
    )
    value_grad = jnp.einsum(
        "bhqk,bqhe->bkhe", soft_low, mixed_grad, preferred_element_type=jnp.float32
    )
    score_grad = soft_probs * (soft_grad - jnp.sum(soft_grad * soft_probs, axis=-1, keepdims=True))
    score_low = score_grad.astype(jnp.bfloat16)
    query_grad = score_scale * jnp.einsum(
        "bhqk,bkhe->bqhe", score_low, key_rows, preferred_element_type=jnp.float32
    )
    key_grad = score_scale * jnp.einsum(
        "bhqk,bqhe->bkhe", score_low, queries, preferred_element_type=jnp.float32
    )
    return (query_grad, key_grad, value_grad)


def block_pieces(tok_rows, gathered):
    qkv_matrix, proj_matrix, up_matrix, down_matrix, vectors = gathered
    columns = vectors.astype(jnp.float32)
    normed_one = layer_norm(tok_rows, columns[:, 0], columns[:, 1]).astype(jnp.bfloat16)
    projected = jnp.dot(normed_one, qkv_matrix, preferred_element_type=jnp.float32)
    width = projected.shape[1] // 3
    queries = (projected[:, :width] + columns[:, 4]).astype(jnp.bfloat16)
    key_rows = projected[:, width : 2 * width].astype(jnp.bfloat16)
    values = (projected[:, 2 * width :] + columns[:, 5]).astype(jnp.bfloat16)
    (mixed_rows,) = over_groups(attend_forward, (queries, key_rows, values))
    mixed_low = mixed_rows.astype(jnp.bfloat16)
    attended = tok_rows + (
        jnp.dot(mixed_low, proj_matrix, preferred_element_type=jnp.float32) + columns[:, 6]
    )
    normed_two = layer_norm(attended, columns[:, 2], columns[:, 3]).astype(jnp.bfloat16)
    up_bias = columns[:, 7:11].T.reshape(-1)
    hidden = jnp.dot(normed_two, up_matrix, preferred_element_type=jnp.float32) + up_bias
    activated = jax.nn.gelu(hidden, approximate=False).astype(jnp.bfloat16)
    output = attended + (
        jnp.dot(activated, down_matrix, preferred_element_type=jnp.float32) + columns[:, 11]
    )
    return (
        output,
        (
            columns,
            normed_one,
            queries,
            key_rows,
            values,
            mixed_low,
            attended,
            normed_two,
            hidden,
            activated,
        ),
    )


def block_backward(tok_rows, gathered, out_grad):
    _, saved = block_pieces(tok_rows, gathered)
    (
        columns,
        normed_one,
        queries,
        key_rows,
        values,
        mixed_low,
        attended,
        normed_two,
        hidden,
        activated,
    ) = saved
    qkv_matrix, proj_matrix, up_matrix, down_matrix, _ = gathered
    out_low = out_grad.astype(jnp.bfloat16)
    down_grad = contract_rows(activated, out_low)
    down_bias_grad = jnp.sum(out_grad, axis=0)
    active_grad = times_transpose(out_low, down_matrix)
    _, gelu_back = jax.vjp(partial(jax.nn.gelu, approximate=False), hidden)
    (hidden_grad,) = gelu_back(active_grad)
    up_bias_grad = jnp.sum(hidden_grad, axis=0)
    hidden_low = hidden_grad.astype(jnp.bfloat16)
    up_grad = contract_rows(normed_two, hidden_low)
    normed_two_grad = times_transpose(hidden_low, up_matrix)
    _, norm_back_two = jax.vjp(layer_norm, attended, columns[:, 2], columns[:, 3])
    attended_part, gain_two_grad, shift_two_grad = norm_back_two(normed_two_grad)
    attended_grad = out_grad + attended_part
    attended_low = attended_grad.astype(jnp.bfloat16)
    proj_bias_grad = jnp.sum(attended_grad, axis=0)
    proj_grad = contract_rows(mixed_low, attended_low)
    mixed_grad = times_transpose(attended_low, proj_matrix).astype(jnp.bfloat16)
    query_grad, key_grad, value_grad = over_groups(
        attend_backward, (queries, key_rows, values, mixed_grad)
    )
    projected_low = jnp.concatenate([query_grad, key_grad, value_grad], axis=1).astype(jnp.bfloat16)
    qkv_grad = contract_rows(normed_one, projected_low)
    normed_one_grad = times_transpose(projected_low, qkv_matrix)
    _, norm_back_one = jax.vjp(layer_norm, tok_rows, columns[:, 0], columns[:, 1])
    input_part, gain_one_grad, shift_one_grad = norm_back_one(normed_one_grad)
    width = tok_rows.shape[1]
    small_grads = jnp.stack(
        [
            gain_one_grad,
            shift_one_grad,
            gain_two_grad,
            shift_two_grad,
            jnp.sum(query_grad, axis=0),
            jnp.sum(value_grad, axis=0),
            proj_bias_grad,
        ],
        axis=1,
    )
    vector_grad = jnp.concatenate(
        [small_grads, up_bias_grad.reshape(4, width).T, down_bias_grad[:, None]], axis=1
    )
    return (attended_grad + input_part, (qkv_grad, proj_grad, up_grad, down_grad, vector_grad))


def shards_of(params, layer_index):
    return tuple((param[layer_index].astype(jnp.bfloat16) for param in params))


def gather_forward(shards):
    column_full = jax.tree.map(
        lambda part, own: part.astype(own.dtype),
        lax.all_gather(as_sent(shards), "fsdp", axis=1, tiled=True),
        shards,
    )
    return jax.tree.map(
        lambda part, own: part.astype(own.dtype),
        lax.all_gather(as_sent(column_full), "dp", axis=0, tiled=True),
        column_full,
    )


def gather_backward(shards):
    column_full = jax.tree.map(
        lambda part, own: part.astype(own.dtype),
        lax.all_gather(as_sent(shards), "fsdp", axis=1, tiled=True),
        shards,
    )
    return jax.tree.map(
        lambda part, own: part.astype(own.dtype),
        lax.all_gather(as_sent(column_full), "dp", axis=0, tiled=True),
        column_full,
    )


def fetch_weights(params, layer_index):
    fetched = gather_backward(shards_of(params, layer_index))
    return fetched


def scatter_gradients(gradients):
    row_owned = (
        lax.psum_scatter(gradients[0], "dp", scatter_dimension=0, tiled=True),
        lax.psum_scatter(gradients[1], "dp", scatter_dimension=0, tiled=True),
        lax.psum_scatter(gradients[2], "dp", scatter_dimension=0, tiled=True),
        lax.psum_scatter(gradients[3], "dp", scatter_dimension=0, tiled=True),
        lax.psum_scatter(gradients[4], "dp", scatter_dimension=0, tiled=True),
    )
    owned = (
        lax.psum_scatter(row_owned[0], "fsdp", scatter_dimension=1, tiled=True),
        lax.psum_scatter(row_owned[1], "fsdp", scatter_dimension=1, tiled=True),
        lax.psum_scatter(row_owned[2], "fsdp", scatter_dimension=1, tiled=True),
        lax.psum_scatter(row_owned[3], "fsdp", scatter_dimension=1, tiled=True),
        lax.psum_scatter(row_owned[4], "fsdp", scatter_dimension=1, tiled=True),
    )
    return owned


def live_rows(count_here, total_rows):
    boundary = VIEWS * GLOB_TOK
    positions = jnp.arange(total_rows, dtype=jnp.int32)
    crop_index = (positions - boundary) // CROP_TOK
    live_mask = jnp.logical_or(positions < boundary, crop_index < count_here)
    return live_mask.astype(jnp.float32)[:, None]


def class_rows(tok_rows):
    boundary = VIEWS * GLOB_TOK
    width = tok_rows.shape[1]
    glob_first = tok_rows[:boundary].reshape(VIEWS, GLOB_TOK, width)[:, 0]
    crop_first = tok_rows[boundary:].reshape(CROPS, CROP_TOK, width)[:, 0]
    return jnp.concatenate([glob_first, crop_first], axis=0)


def add_class_rows(tok_rows, returned):
    boundary = VIEWS * GLOB_TOK
    width = tok_rows.shape[1]
    glob_part = tok_rows[:boundary].reshape(VIEWS, GLOB_TOK, width).at[:, 0].add(returned[:VIEWS])
    crop_part = tok_rows[boundary:].reshape(CROPS, CROP_TOK, width).at[:, 0].add(returned[VIEWS:])
    return jnp.concatenate(
        [glob_part.reshape(boundary, width), crop_part.reshape(CROPS * CROP_TOK, width)], axis=0
    )


def adamw(weight, first_moment, second, gradient, decay_factor, rate):
    new_first = beta_one * first_moment + (1.0 - beta_one) * gradient
    new_second = beta_two * second + (1.0 - beta_two) * gradient * gradient
    first_hat = new_first / (1.0 - beta_one**STEP)
    second_hat = new_second / (1.0 - beta_two**STEP)
    new_weight = weight - rate * (
        first_hat / (jnp.sqrt(second_hat) + adam_epsilon) + decay_factor * weight_decay * weight
    )
    return (new_weight, new_first, new_second)


def local(
    tokens,
    focal_count,
    cls_order,
    out_cotangent,
    cls_cotangent,
    qkv_weight,
    proj_weight,
    fc1_weight,
    fc2_weight,
    vec_params,
    qkv_first,
    proj_first,
    fc1_first,
    fc2_first,
    vec_first,
    qkv_second,
    proj_second,
    fc1_second,
    fc2_second,
    vec_second,
):
    params = (qkv_weight, proj_weight, fc1_weight, fc2_weight, vec_params)
    rows_input = tokens[0, 0].astype(jnp.float32)
    first_full = gather_forward(shards_of(params, 0))
    middle, _ = block_pieces(rows_input, first_full)
    second_full = gather_forward(shards_of(params, 1))
    final_rows, _ = block_pieces(middle, second_full)
    live_mask = live_rows(focal_count[0, 0], final_rows.shape[0])
    shown_rows = (final_rows * live_mask).astype(jnp.bfloat16)
    heads_rows = class_rows(shown_rows)
    pooled = lax.all_gather(heads_rows, "dp", axis=0, tiled=True)
    picker = (
        cls_order[0][:, None] == jnp.arange(pooled.shape[0], dtype=jnp.int32)[None, :]
    ).astype(jnp.bfloat16)
    regrouped = jnp.dot(picker, pooled, preferred_element_type=jnp.float32).astype(jnp.bfloat16)
    class_grad = cls_cotangent[0, 0]
    returned = lax.psum_scatter(
        contract_rows(picker, class_grad), "dp", scatter_dimension=0, tiled=True
    )
    final_grad = add_class_rows(out_cotangent[0, 0].astype(jnp.float32), returned) * live_mask
    middle_grad, grads_second = block_backward(middle, fetch_weights(params, 1), final_grad)
    owned_second = scatter_gradients(grads_second)
    input_grad, grads_first = block_backward(rows_input, fetch_weights(params, 0), middle_grad)
    owned_first = scatter_gradients(grads_first)
    gradients = [
        jnp.stack([lower_part, upper_part])
        for lower_part, upper_part in zip(owned_first, owned_second)
    ]
    firsts = (qkv_first, proj_first, fc1_first, fc2_first, vec_first)
    seconds = (qkv_second, proj_second, fc1_second, fc2_second, vec_second)
    decay_flags = (1.0, 1.0, 1.0, 1.0, 0.0)
    rates = (step_rate, step_rate, step_rate, step_rate, vector_rate)
    updated = [
        adamw(param, first_moment, second, gradient, flag, rate)
        for param, first_moment, second, gradient, flag, rate in zip(
            params, firsts, seconds, gradients, decay_flags, rates
        )
    ]
    return (
        shown_rows[None, None],
        regrouped[None, None],
        input_grad[None, None],
        updated[0][0],
        updated[1][0],
        updated[2][0],
        updated[3][0],
        updated[4][0],
        updated[0][1],
        updated[1][1],
        updated[2][1],
        updated[3][1],
        updated[4][1],
        updated[0][2],
        updated[1][2],
        updated[2][2],
        updated[3][2],
        updated[4][2],
    )


def solution(mesh):
    return jax.shard_map(
        local,
        mesh=mesh,
        in_specs=(
            P("dp", "fsdp", None, None),
            P("dp", "fsdp"),
            P("fsdp", "dp"),
            P("dp", "fsdp", None, None),
            P("dp", "fsdp", None, None),
            P(None, "dp", "fsdp"),
            P(None, "dp", "fsdp"),
            P(None, "dp", "fsdp"),
            P(None, "dp", "fsdp"),
            P(None, "dp", "fsdp"),
            P(None, "dp", "fsdp"),
            P(None, "dp", "fsdp"),
            P(None, "dp", "fsdp"),
            P(None, "dp", "fsdp"),
            P(None, "dp", "fsdp"),
            P(None, "dp", "fsdp"),
            P(None, "dp", "fsdp"),
            P(None, "dp", "fsdp"),
            P(None, "dp", "fsdp"),
            P(None, "dp", "fsdp"),
        ),
        out_specs=(
            P("dp", "fsdp", None, None),
            P("dp", "fsdp", None, None),
            P("dp", "fsdp", None, None),
            P(None, "dp", "fsdp"),
            P(None, "dp", "fsdp"),
            P(None, "dp", "fsdp"),
            P(None, "dp", "fsdp"),
            P(None, "dp", "fsdp"),
            P(None, "dp", "fsdp"),
            P(None, "dp", "fsdp"),
            P(None, "dp", "fsdp"),
            P(None, "dp", "fsdp"),
            P(None, "dp", "fsdp"),
            P(None, "dp", "fsdp"),
            P(None, "dp", "fsdp"),
            P(None, "dp", "fsdp"),
            P(None, "dp", "fsdp"),
            P(None, "dp", "fsdp"),
        ),
        check_vma=False,
    )
```

profile of v0, /device:TPU:0, one launch (start us, length us, event | category | flops | bytes accessed | tf_op | source)
XLA Modules:
  0.0 1458.9 jit_solution(12057623073326390891)
XLA Ops:
  46.2 31.3 %all-gather.11 = bf16[1,384,12]{2,0,1:T(2,128)(2,1)S(1)} all-gather(bf16[1,48,12]{2,0,1:T(2,128)(2,1)S(1)} %copy.376), channel_id=13, replica_groups=mesh['dp'=8,'fsdp'=4] {'dp'}, dimensions={1}, use_global_device_ids=true | all-gather | bytes 10368 | tf_op jit(solution)/shard_map/all_gather | solution.py:211
  84.2 30.9 %all-gather.1 = bf16[1,384,12]{2,0,1:T(2,128)(2,1)S(1)} all-gather(bf16[1,48,12]{2,0,1:T(2,128)(2,1)S(1)} %copy.354), channel_id=3, replica_groups=mesh['dp'=8,'fsdp'=4] {'dp'}, dimensions={1}, use_global_device_ids=true | all-gather | bytes 10368 | tf_op jit(solution)/shard_map/all_gather | solution.py:211
  133.0 33.7 %all-gather.3 = bf16[1,384,1152]{2,1,0:T(8,128)(2,1)S(1)} all-gather(bf16[1,48,1152]{2,1,0:T(8,128)(2,1)} %copy.357), channel_id=5, replica_groups=mesh['dp'=8,'fsdp'=4] {'dp'}, dimensions={1}, use_global_device_ids=true | all-gather | bytes 995328 | tf_op jit(solution)/shard_map/all_gather | solution.py:211
  197.8 33.3 %all-gather.5 = bf16[1,384,384]{2,1,0:T(8,128)(2,1)} all-gather(bf16[1,48,384]{2,1,0:T(8,128)(2,1)} %copy.373), channel_id=7, replica_groups=mesh['dp'=8,'fsdp'=4] {'dp'}, dimensions={1}, use_global_device_ids=true | all-gather | bytes 331776 | tf_op jit(solution)/shard_map/all_gather | solution.py:211
  231.1 33.4 %all-gather.15 = bf16[1,384,384]{2,1,0:T(8,128)(2,1)} all-gather(bf16[1,48,384]{2,1,0:T(8,128)(2,1)} %copy.393), channel_id=17, replica_groups=mesh['dp'=8,'fsdp'=4] {'dp'}, dimensions={1}, use_global_device_ids=true | all-gather | bytes 331776 | tf_op jit(solution)/shard_map/all_gather | solution.py:211
  264.6 8.4 all-gather.12
  274.8 34.3 %all-gather.13 = bf16[1,384,1152]{2,1,0:T(8,128)(2,1)} all-gather(bf16[1,48,1152]{2,1,0:T(8,128)(2,1)} %copy.378), channel_id=15, replica_groups=mesh['dp'=8,'fsdp'=4] {'dp'}, dimensions={1}, use_global_device_ids=true | all-gather | bytes 995328 | tf_op jit(solution)/shard_map/all_gather | solution.py:211
  375.1 26.3 %multiply_convert_fusion.1 = (bf16[1528,1536]{1,0:T(8,128)(2,1)}, f32[1528,1536]{1,0:T(8,128)}, f32[1528,1536]{1,0:T(8,128)}) fusion(f32[1536]{0:T(1024)S(1)} %copy-done.117, bf16[1,384,1536]{2,1,0:T(8,128)(2,1)} %all-gather.25.cloned.1.call-done, f32[1528,384]{1,0:T(8,128)S(1)} %get-tuple-element.198, f32[384]{0:T(512)S(1)} %copy-done.120, ...), kind=kOutput, calls=%fused_computation.25 | convolution fusion | flops 1960338432 | bytes 27018176 | tf_op jit(solution)/shard_map/dot_general | solution.py:118
  475.0 26.8 %multiply_convert_fusion = (bf16[1528,1536]{1,0:T(8,128)(2,1)}, f32[1528,1536]{1,0:T(8,128)}, f32[1528,1536]{1,0:T(8,128)}) fusion(f32[1536]{0:T(1024)S(1)} %copy-done.116, bf16[1,384,1536]{2,1,0:T(8,128)(2,1)} %all-gather.29.cloned.1.call-done, f32[1528,384]{1,0:T(8,128)} %copy-done.8, f32[384]{0:T(512)S(1)} %copy-done.121, f32[384]{0:T(512)S(1)} %copy-done.108, ...), kind=kOutput, calls=%fused_computation.12 | convolution fusion | flops 1960338432 | bytes 27018176 | tf_op jit(solution)/shard_map/dot_general | solution.py:118
  501.7 11.2 fusion.211
  598.7 11.0 multiply_reduce_fusion.7
  612.8 10.5 fusion.212
  687.2 11.7 fusion.178
  720.8 11.9 fusion.171
  782.0 15.7 %fusion.183 = (f32[384]{0:T(512)}, f32[1528]{0:T(1024)S(1)}, f32[1528,384]{1,0:T(8,128)}) fusion(f32[384]{0:T(512)S(1)} %copy-done.89, f32[1528]{0:T(1024)S(1)} %copy-done.63, bf16[1,1,1528,384]{3,2,1,0:T(8,128)(2,1)S(1)} %copy-done.3, bf16[1,384,1152]{2,1,0:T(8,128)(2,1)S(1)} %copy-done.34, bf16[740,384]{0,1:T(8,128)(2,1)} %reshape.613, ...), kind=kOutput, calls=%fused_computation.351 | convolution fusion | flops 1376518272 | bytes 7941056 | tf_op jit(solution)/shard_map/dot_general | solution.py:48
  831.8 15.9 %reduce-scatter.35.cloned.1.call-done = f32[48,1152]{1,0:T(8,128)} async-done(((f32[384,1152]{1,0:T(8,128)}), f32[48,1152]{1,0:T(8,128)}) %reduce-scatter.35.cloned.1.call-update) | async-done | bytes 221200 | tf_op jit(solution)/shard_map/reduce_scatter | solution.py:236
  851.7 67.8 %reduce-scatter.53.cloned.1.call-done = f32[192,384]{1,0:T(8,128)} async-done(((f32[1536,384]{1,0:T(8,128)}), f32[192,384]{1,0:T(8,128)}) %reduce-scatter.53.cloned.1.call-update) | async-done | bytes 294928 | tf_op jit(solution)/shard_map/reduce_scatter | solution.py:239
  937.4 54.1 %reduce-scatter.51.cloned.1.call-done = f32[192,384]{1,0:T(8,128)} async-done(((f32[1536,384]{1,0:T(8,128)}), f32[192,384]{1,0:T(8,128)}) %reduce-scatter.51.cloned.1.call-update) | async-done | bytes 294928 | tf_op jit(solution)/shard_map/reduce_scatter | solution.py:239
  997.6 66.0 %reduce-scatter.47.cloned.1.call-done = f32[48,1536]{1,0:T(8,128)} async-done(((f32[384,1536]{1,0:T(8,128)}), f32[48,1536]{1,0:T(8,128)}) %reduce-scatter.47.cloned.1.call-update) | async-done | bytes 294928 | tf_op jit(solution)/shard_map/reduce_scatter | solution.py:238
  1064.6 30.6 %all_gather.103 = bf16[192,384]{1,0:T(8,128)(2,1)S(1)} all-gather(bf16[24,384]{1,0:T(8,128)(2,1)S(1)} %pad_maximum_fusion.16), channel_id=1, replica_groups=mesh['dp'=8,'fsdp'=4] {'dp'}, dimensions={0}, use_global_device_ids=true | all-gather | bytes 165888 | tf_op jit(solution)/shard_map/all_gather | solution.py:320
  1096.7 31.3 %reduce-scatter.69.cloned.1.call-done = f32[48,12]{1,0:T(8,128)} async-done(((f32[384,12]{1,0:T(8,128)}), f32[48,12]{1,0:T(8,128)}) %reduce-scatter.69.cloned.1.call-update) | async-done | bytes 2320
  1128.8 62.7 %reduce-scatter.67.cloned.1.call-done = f32[48,12]{1,0:T(8,128)} async-done(((f32[384,12]{1,0:T(8,128)}), f32[48,12]{1,0:T(8,128)}) %reduce-scatter.67.cloned.1.call-update) | async-done | bytes 2320
  1192.3 10.1 all-reduce.3
  1205.0 8.3 reduce-scatter.61.cloned.1.call-done
  1214.1 21.9 %reduce-scatter.59.cloned.1.call-done = f32[96,48]{1,0:T(8,128)} async-done(((f32[384,48]{1,0:T(8,128)}), f32[96,48]{1,0:T(8,128)}) %reduce-scatter.59.cloned.1.call-update) | async-done | bytes 18448
  1236.9 72.5 %reduce-scatter.43.cloned.1.call-done = f32[48,1536]{1,0:T(8,128)} async-done(((f32[384,1536]{1,0:T(8,128)}), f32[48,1536]{1,0:T(8,128)}) %reduce-scatter.43.cloned.1.call-update) | async-done | bytes 294928 | tf_op jit(solution)/shard_map/reduce_scatter | solution.py:238
  1310.9 22.1 %reduce-scatter.57.cloned.1.call-done = f32[288,48]{1,0:T(8,128)} async-done(((f32[1152,48]{1,0:T(8,128)}), f32[288,48]{1,0:T(8,128)}) %reduce-scatter.57.cloned.1.call-update) | async-done | bytes 55312
  1334.0 23.7 %reduce-scatter.55.cloned.1.call-done = f32[288,48]{1,0:T(8,128)} async-done(((f32[1152,48]{1,0:T(8,128)}), f32[288,48]{1,0:T(8,128)}) %reduce-scatter.55.cloned.1.call-update) | async-done | bytes 55312
  1360.7 20.4 %reduce-scatter.65.cloned.1.call-done = f32[96,192]{1,0:T(8,128)} async-done(((f32[384,192]{1,0:T(8,128)}), f32[96,192]{1,0:T(8,128)}) %reduce-scatter.65.cloned.1.call-update) | async-done | bytes 73744
  1382.1 22.5 %reduce-scatter.63.cloned.1.call-done = f32[96,192]{1,0:T(8,128)} async-done(((f32[384,192]{1,0:T(8,128)}), f32[96,192]{1,0:T(8,128)}) %reduce-scatter.63.cloned.1.call-update) | async-done | bytes 73744
  1406.5 21.0 %reduce-scatter.49.cloned.1.call-done = f32[48,384]{1,0:T(8,128)} async-done(((f32[48,1536]{1,0:T(8,128)}), f32[48,384]{1,0:T(8,128)}) %reduce-scatter.49.cloned.1.call-update) | async-done | bytes 73744 | tf_op jit(solution)/shard_map/reduce_scatter | solution.py:245
  1427.5 22.8 %reduce-scatter.45.cloned.1.call-done = f32[48,384]{1,0:T(8,128)} async-done(((f32[48,1536]{1,0:T(8,128)}), f32[48,384]{1,0:T(8,128)}) %reduce-scatter.45.cloned.1.call-update) | async-done | bytes 73744 | tf_op jit(solution)/shard_map/reduce_scatter | solution.py:245
  (589 shorter events, 536.6 us)
Async XLA Ops:
  7.2 356.3 %all-reduce.6.cloned.1.call-start = ((), (), s32[]{:S(2)}) async-start(), calls=%async_computation.40 | async-start | bytes 589824
  9.6 365.4 %all-gather.25.cloned.1.call-start = ((), (), s32[]{:S(2)}) async-start(), calls=%async_computation.28 | async-start | bytes 1327104 | tf_op jit(solution)/shard_map/all_gather | solution.py:211
  17.7 98.7 %copy-start.29 = (bf16[1,1,1528,384]{3,2,1,0:T(8,128)(2,1)S(1)}, bf16[1,1,1528,384]{3,2,1,0:T(8,128)(2,1)}, u32[]{:S(2)}) copy-start(bf16[1,1,1528,384]{3,2,1,0:T(8,128)(2,1)} %param.27) | copy-start | bytes 3520516
  17.7 383.7 %all-gather.27.cloned.1.call-start = ((), (), s32[]{:S(2)}) async-start(), calls=%async_computation.29 | async-start | bytes 1327104 | tf_op jit(solution)/shard_map/all_gather | solution.py:211
  27.1 447.8 %all-gather.29.cloned.1.call-start = ((), (), s32[]{:S(2)}) async-start(), calls=%async_computation.30 | async-start | bytes 1327104 | tf_op jit(solution)/shard_map/all_gather | solution.py:211
  33.1 468.6 %all-gather.31.cloned.1.call-start = ((), (), s32[]{:S(2)}) async-start(), calls=%async_computation.31 | async-start | bytes 1327104 | tf_op jit(solution)/shard_map/all_gather | solution.py:211
  40.9 778.3 %reduce-scatter.41.cloned.1.call-start = ((), (), s32[]{:S(2)}) async-start(), calls=%async_computation.21 | async-start | bytes 663552 | tf_op jit(solution)/shard_map/reduce_scatter | solution.py:237
  560.5 260.5 %reduce-scatter.39.cloned.1.call-start = ((), (), s32[]{:S(2)}) async-start(), calls=%async_computation.20 | async-start | bytes 663552 | tf_op jit(solution)/shard_map/reduce_scatter | solution.py:237
  647.5 182.2 %reduce-scatter.37.cloned.1.call-start = ((), (), s32[]{:S(2)}) async-start(), calls=%async_computation.19 | async-start | bytes 1990656 | tf_op jit(solution)/shard_map/reduce_scatter | solution.py:236
  698.9 148.8 %reduce-scatter.35.cloned.1.call-start = ((), (), s32[]{:S(2)}) async-start(), calls=%async_computation.18 | async-start | bytes 1990656 | tf_op jit(solution)/shard_map/reduce_scatter | solution.py:236
  732.7 186.8 %reduce-scatter.53.cloned.1.call-start = ((), (), s32[]{:S(2)}) async-start(), calls=%async_computation.27 | async-start | bytes 2654208 | tf_op jit(solution)/shard_map/reduce_scatter | solution.py:239
  739.8 251.7 %reduce-scatter.51.cloned.1.call-start = ((), (), s32[]{:S(2)}) async-start(), calls=%async_computation.26 | async-start | bytes 2654208 | tf_op jit(solution)/shard_map/reduce_scatter | solution.py:239
  748.0 315.7 %reduce-scatter.47.cloned.1.call-start = ((), (), s32[]{:S(2)}) async-start(), calls=%async_computation.24 | async-start | bytes 2654208 | tf_op jit(solution)/shard_map/reduce_scatter | solution.py:238
  755.6 372.4 %reduce-scatter.69.cloned.1.call-start = ((), (), s32[]{:S(2)}) async-start(), calls=%async_computation.39 | async-start | bytes 221184
  797.7 393.8 %reduce-scatter.67.cloned.1.call-start = ((), (), s32[]{:S(2)}) async-start(), calls=%async_computation.38 | async-start | bytes 221184
  819.1 394.2 %reduce-scatter.61.cloned.1.call-start = ((), (), s32[]{:S(2)}) async-start(), calls=%async_computation.35 | async-start | bytes 245760
  820.9 415.2 %reduce-scatter.59.cloned.1.call-start = ((), (), s32[]{:S(2)}) async-start(), calls=%async_computation.34 | async-start | bytes 245760
  822.7 486.7 %reduce-scatter.43.cloned.1.call-start = ((), (), s32[]{:S(2)}) async-start(), calls=%async_computation.22 | async-start | bytes 2654208 | tf_op jit(solution)/shard_map/reduce_scatter | solution.py:238
  829.7 503.4 %reduce-scatter.57.cloned.1.call-start = ((), (), s32[]{:S(2)}) async-start(), calls=%async_computation.33 | async-start | bytes 737280
  831.8 526.0 %reduce-scatter.55.cloned.1.call-start = ((), (), s32[]{:S(2)}) async-start(), calls=%async_computation.32 | async-start | bytes 737280
  849.7 531.4 %reduce-scatter.65.cloned.1.call-start = ((), (), s32[]{:S(2)}) async-start(), calls=%async_computation.37 | async-start | bytes 491520
  921.4 483.2 %reduce-scatter.63.cloned.1.call-start = ((), (), s32[]{:S(2)}) async-start(), calls=%async_computation.36 | async-start | bytes 491520
  993.4 209.1 %copy-start.105 = (f32[2,48,3]{1,0,2:T(2,128)S(1)}, f32[2,48,3]{1,0,2:T(2,128)}, u32[]{:S(2)}) copy-start(f32[2,48,3]{1,0,2:T(2,128)} %param.33) | copy-start | bytes 3460
  993.4 434.1 %reduce-scatter.49.cloned.1.call-start = ((), (), s32[]{:S(2)}) async-start(), calls=%async_computation.25 | async-start | bytes 368640 | tf_op jit(solution)/shard_map/reduce_scatter | solution.py:245
  997.6 408.0 %copy-start.56 = (f32[2,192,96]{2,1,0:T(8,128)S(1)}, f32[2,192,96]{2,1,0:T(8,128)}, u32[]{:S(2)}) copy-start(f32[2,192,96]{2,1,0:T(8,128)} %param.32) | copy-start | bytes 442372
  997.6 408.0 %copy-start.74 = (f32[2,192,96]{2,1,0:T(8,128)S(1)}, f32[2,192,96]{2,1,0:T(8,128)}, u32[]{:S(2)}) copy-start(f32[2,192,96]{2,1,0:T(8,128)} %param.37) | copy-start | bytes 442372
  997.6 408.0 %copy-start.75 = (f32[2,192,96]{2,1,0:T(8,128)S(1)}, f32[2,192,96]{2,1,0:T(8,128)}, u32[]{:S(2)}) copy-start(f32[2,192,96]{2,1,0:T(8,128)} %param.42) | copy-start | bytes 442372
  1063.6 386.7 %copy-start.60 = (f32[2,48,384]{2,1,0:T(8,128)S(1)}, f32[2,48,384]{2,1,0:T(8,128)}, u32[]{:S(2)}) copy-start(f32[2,48,384]{2,1,0:T(8,128)} %param.31) | copy-start | bytes 442372
  1063.7 386.7 %copy-start.76 = (f32[2,48,384]{2,1,0:T(8,128)S(1)}, f32[2,48,384]{2,1,0:T(8,128)}, u32[]{:S(2)}) copy-start(f32[2,48,384]{2,1,0:T(8,128)} %param.36) | copy-start | bytes 442372
  1063.7 386.7 %copy-start.77 = (f32[2,48,384]{2,1,0:T(8,128)S(1)}, f32[2,48,384]{2,1,0:T(8,128)}, u32[]{:S(2)}) copy-start(f32[2,48,384]{2,1,0:T(8,128)} %param.41) | copy-start | bytes 442372
  1063.7 386.7 %reduce-scatter.45.cloned.1.call-start = ((), (), s32[]{:S(2)}) async-start(), calls=%async_computation.23 | async-start | bytes 368640 | tf_op jit(solution)/shard_map/reduce_scatter | solution.py:245
  1309.4 142.7 %copy-start.1 = (bf16[1,1,24,384]{3,2,1,0:T(8,128)(2,1)S(1)}, bf16[1,1,24,384]{3,2,1,0:T(8,128)(2,1)}, u32[]{:S(2)}) copy-start(bf16[1,1,24,384]{3,2,1,0:T(8,128)(2,1)} %param.28) | copy-start | bytes 55300
  (124 other events, 1068.3 us)
Sparse Core Ops, SparseCore 0:
  11.4 73.5 all-reduce.5
  87.4 40.3 all-gather.24
  130.8 44.7 all-gather.26
  177.9 40.1 all-gather.28
  220.9 41.8 all-gather.30
  560.6 62.8 reduce-scatter.40
  647.7 62.9 reduce-scatter.38
  714.5 64.9 reduce-scatter.36
  782.9 64.7 reduce-scatter.34
  851.4 67.9 reduce-scatter.52
  923.4 68.0 reduce-scatter.50
  995.3 68.2 reduce-scatter.46
  1067.8 60.1 reduce-scatter.68
  1131.4 60.0 reduce-scatter.66
  1194.5 18.7 reduce-scatter.60
  1216.3 19.6 reduce-scatter.58
  1239.8 69.5 reduce-scatter.42
  1311.9 21.1 reduce-scatter.56
  1335.7 22.0 reduce-scatter.54
  1360.3 20.7 reduce-scatter.64
  1383.7 20.8 reduce-scatter.62
  1407.2 20.2 reduce-scatter.48
  1430.0 20.2 reduce-scatter.44
where the time goes:
time: 1470 us; the launch traced here: 1460 us
  waiting for transfers between devices  534 us (36%)
  blocking collectives  304 us (21%)
  local copies, waits for them, and re-layouts  269 us (18%)
  matrix products  267 us (18%)
  other arithmetic  65.3 us (4%)
  between operations  18 us (1%)
    unnamed x32, waiting for transfers between devices  213 us
    all_gather x6, blocking collectives, gather_forward(): lax.all_gather(as_sent(column_full), 'dp', axis=0, tiled=True)  197 us
    reduce_scatter x2, waiting for transfers between devices, scatter_gradients(): lax.psum_scatter(gradients[2], 'dp', scatter_dimension=0, tiled=True)  139 us
    reduce_scatter x2, waiting for transfers between devices, scatter_gradients(): lax.psum_scatter(gradients[3], 'dp', scatter_dimension=0, tiled=True)  122 us
    all_gather x10, blocking collectives, gather_forward(): lax.all_gather(as_sent(shards), 'fsdp', axis=1, tiled=True)  66 us
    reshape x16, local copies, waits for them, and re-layouts, over_groups(): second_out.reshape(CROPS * CROP_TOK, -1)  61.7 us
    dot_general x8, matrix products, times_transpose(): lax.dot_general(left_side, right_side, (((1,), (1,)), ((), ())), preferre...  59.9 us
    dot_general x9, matrix products, contract_rows(): lax.dot_general(left_side, right_side, (((0,), (0,)), ((), ())), preferre...  56.2 us
  transfers between devices with their start and end apart: 23, of which 15 were waited for; matrix products, arithmetic and copies ran while one was open for 36% of the time, Pallas kernels for 0%

commit v1 on v0

v1 whole, which is shorter than its diff:
```python
import jax
import jax.numpy as jnp
import numpy as np
from jax import lax
from jax.experimental import pallas as pl
from jax.experimental.pallas import tpu as pltpu
from jax.sharding import PartitionSpec as P

D = 384
HEADS = 6
HEAD_DIM = 64
FF = 1536
GLOB_TOK = 197
CROP_TOK = 37
STEP = 5
VIEWS = 4
CROPS = 20
CROP_GROUP = 5
GROUPS = CROPS // CROP_GROUP
TILE = 208
TILES = VIEWS + GROUPS
ROWS = TILE * TILES
PER_STEP = 2
CHUNK = TILE * PER_STEP
STEPS = TILES // PER_STEP
CLS_DEV = VIEWS + CROPS
TOK_DEV = VIEWS * GLOB_TOK + CROPS * CROP_TOK
CLS_PAD = 32
SHARD = 48
PACKS = 3
SUB = 64
WIDE_SUB = 64
SLOTS = 3
WIDE = 1552
GATHERED = (2, 2, 4, 2, SHARD, D)
SPLIT = (PACKS, *GATHERED)

beta_one = 0.5
beta_two = 0.5
step_rate = 0.03
vector_rate = 0.4
weight_decay = 0.05
adam_epsilon = 1e-08
norm_epsilon = 1e-06
score_scale = HEAD_DIM ** (-0.5)

BF16 = jnp.bfloat16
F32 = jnp.float32
VMEM_LIMIT = 60 * 1024 * 1024
MESH = pl.DeviceIdType.MESH


def dot(left, right):
    return lax.dot_general(left, right, (((1,), (0,)), ((), ())), preferred_element_type=F32)


def dot_t(left, right):
    return lax.dot_general(left, right, (((1,), (1,)), ((), ())), preferred_element_type=F32)


def normalise(rows):
    centre = jnp.mean(rows, axis=-1, keepdims=True)
    centred = rows - centre
    variance = jnp.mean(centred * centred, axis=-1, keepdims=True)
    spread = lax.rsqrt(variance + norm_epsilon)
    return centred * spread, spread


def norm_back(grad, unit, spread, gain):
    scaled = grad * gain
    return spread * (
        scaled
        - jnp.mean(scaled, axis=-1, keepdims=True)
        - unit * jnp.mean(scaled * unit, axis=-1, keepdims=True)
    )


def gelu_pair(z):
    t = 1.0 / (1.0 + 0.23164189 * jnp.abs(z))
    bell = jnp.exp2(z * z * -0.72134752)
    poly = t * (
        0.127414796 + t * (-0.142248368 + t * (0.7107068705 + t * (-0.7265760135 + t * 0.5307027145)))
    )
    tail = poly * bell
    phi = jnp.where(z >= 0.0, 1.0 - tail, tail)
    return z * phi, phi + z * (bell * 0.3989422804)


def blocks(total, size):
    return [slice(start, min(start + size, total)) for start in range(0, total, size)]


def fold(value):
    return jnp.sum(value.reshape(value.shape[0] // 8, 8, value.shape[1]), axis=0)


def staged(count, stages):
    for turn in range(count + len(stages) - 1):
        for late, stage in enumerate(stages):
            if 0 <= turn - late < count:
                stage(turn - late)


def add_row(vg_ref, row, value, cols=slice(None)):
    vg_ref[row : row + 1, cols] += jnp.sum(value, axis=0, keepdims=True)


def attend_chunk(h_ref, bias_ref, weights, vec_ref, saved, score_ref, put_mid, unit_ref=None):
    wq, wp = weights
    a1_ref, qkv_ref, pt_ref, o_ref = saved
    total = h_ref.shape[0]
    for at in blocks(total, SUB):
        unit = normalise(h_ref[at, :].astype(F32))[0] if unit_ref is None else unit_ref[at, :]
        a1_ref[at, :] = (unit * vec_ref[0:1, :] + vec_ref[1:2, :]).astype(BF16)
    edges = (0, 512, 1024, 1152)
    made = {}

    def project(part):
        made[part] = dot_t(a1_ref[...], wq[edges[part] : edges[part + 1], :])

    def settle(part):
        for lane in range(edges[part], edges[part + 1], 128):
            cols = slice(lane, lane + 128)
            kind, own = lane // D, slice(lane % D, lane % D + 128)
            for at in blocks(total, WIDE_SUB):
                piece = made[part][at, lane - edges[part] : lane - edges[part] + 128]
                if kind == 0:
                    piece = (piece + vec_ref[4:5, own]).astype(BF16) * score_scale
                elif kind == 2:
                    piece = piece + vec_ref[5:6, own]
                qkv_ref[at, cols] = piece.astype(BF16)

    staged(3, (project, settle))

    low_half = lax.broadcasted_iota(jnp.int32, (TILE, 128), 1) < HEAD_DIM
    items = [(tile, pair) for tile in range(total // TILE) for pair in range(HEADS // 2)]

    def score(index):
        tile, pair = items[index]
        at = slice(tile * TILE, (tile + 1) * TILE)
        q = qkv_ref[at, pair * 128 : pair * 128 + 128]
        k = qkv_ref[at, D + pair * 128 : D + pair * 128 + 128]
        zero = jnp.zeros_like(k)
        both = jnp.concatenate([jnp.where(low_half, k, zero), jnp.where(low_half, zero, k)], axis=0)
        score_ref[index % SLOTS] = dot_t(both, q)

    def soften(index):
        tile, pair = items[index]
        for side in range(2):
            head = tile * HEADS + pair * 2 + side
            for half in blocks(TILE, 128):
                piece = score_ref[index % SLOTS, side * TILE : (side + 1) * TILE, half] + bias_ref[0, :, half]
                top = jnp.max(piece, axis=0, keepdims=True)
                raised = jnp.exp(piece - top)
                share = 1.0 / jnp.sum(raised, axis=0, keepdims=True)
                pt_ref[head, :, half] = (raised * share).astype(BF16)

    def mix(index):
        tile, pair = items[index]
        at = slice(tile * TILE, (tile + 1) * TILE)
        vt = qkv_ref[at, 2 * D + pair * 128 : 2 * D + pair * 128 + 128].T
        head = tile * HEADS + pair * 2
        parts = [
            dot(vt[side * HEAD_DIM : (side + 1) * HEAD_DIM, :], pt_ref[head + side]) for side in range(2)
        ]
        o_ref[at, pair * 128 : pair * 128 + 128] = jnp.concatenate(parts, axis=0).T.astype(BF16)

    staged(len(items), (score, soften, mix))
    attended = dot_t(o_ref[...], wp[...])
    for at in blocks(total, SUB):
        h1 = h_ref[at, :].astype(F32) + (attended[at] + vec_ref[6:7, :])
        unit, _ = normalise(h1)
        put_mid(at, h1, (unit * vec_ref[2:3, :] + vec_ref[3:4, :]).astype(BF16))


def expand_chunk(h1_ref, a2_ref, weights, vec_ref, saved, finish):
    w1, w2 = weights
    u_ref, gp_ref = saved
    total = h1_ref.shape[0]
    totals = []
    made = {}

    def up(part):
        made[part] = dot(a2_ref[...], w1[:, part * 256 : (part + 1) * 256])

    def bend(part):
        for lane in range(part * 256, (part + 1) * 256, 128):
            cols, row = slice(lane, lane + 128), 7 + lane // D
            own = slice(lane % D, lane % D + 128)
            for at in blocks(total, WIDE_SUB):
                z = made[part][at, lane - part * 256 : lane - part * 256 + 128] + vec_ref[row : row + 1, own]
                u, slope = gelu_pair(z)
                u_ref[at, cols] = u.astype(BF16)
                gp_ref[at, cols] = slope.astype(BF16)

    def down(part):
        if part % 3 == 2:
            wide = slice((part - 2) * 256, (part + 1) * 256)
            totals.append(dot_t(u_ref[:, wide], w2[:, wide]))

    staged(6, (up, bend, down))
    for at in blocks(total, SUB):
        finish(at, h1_ref[at, :] + (totals[0][at] + totals[1][at] + vec_ref[11:12, :]))


def forward_chunk(h_ref, bias_ref, weights, vec_ref, saved, spare, finish):
    wq, wp, w1, w2 = weights
    a1_ref, qkv_ref, pt_ref, o_ref, h1_ref, a2_ref, u_ref, gp_ref = saved

    def put_mid(at, h1, a2):
        h1_ref[at, :] = h1
        a2_ref[at, :] = a2

    attend_chunk(h_ref, bias_ref, (wq, wp), vec_ref, (a1_ref, qkv_ref, pt_ref, o_ref), spare[0], put_mid)
    expand_chunk(h1_ref, a2_ref, (w1, w2), vec_ref, (u_ref, gp_ref), finish)


def expand_back(dy_at, weights, vec_ref, saved, grads, vg_ref):
    wp, w1, w2 = weights
    h1_ref, gp_ref = saved
    dy_ref, dz_ref, dh_ref, dol_ref, keep_ref = grads
    size = h1_ref.shape[0]
    total = jnp.zeros((8, D), F32)
    for at in blocks(size, SUB):
        dy = dy_at(at)
        dy_ref[at, :] = dy.astype(BF16)
        total = total + fold(dy)
    add_row(vg_ref, 11, total)
    da2 = []
    made = {}

    def up(part):
        made[part] = dot(dy_ref[...], w2[:, part * 256 : (part + 1) * 256])

    def bend(part):
        for lane in range(part * 256, (part + 1) * 256, 128):
            cols = slice(lane, lane + 128)
            for at in blocks(size, WIDE_SUB):
                du = made[part][at, lane - part * 256 : lane - part * 256 + 128]
                dz_ref[at, cols] = (du * gp_ref[at, cols].astype(F32)).astype(BF16)

    def down(part):
        if part % 3 == 2:
            wide = slice((part - 2) * 256, (part + 1) * 256)
            da2.append(dot_t(dz_ref[:, wide], w1[:, wide]))

    staged(6, (up, bend, down))
    totals = [jnp.zeros((8, D), F32) for _ in range(2)]
    for at in blocks(size, SUB):
        unit, spread = normalise(h1_ref[at, :])
        grad = da2[0][at] + da2[1][at]
        dh1 = dy_at(at) + norm_back(grad, unit, spread, vec_ref[2:3, :])
        keep_ref[at, :] = dh1
        dh_ref[at, :] = dh1.astype(BF16)
        totals = [old + fold(new) for old, new in zip(totals, (grad * unit, grad))]
    add_row(vg_ref, 2, totals[0])
    add_row(vg_ref, 3, totals[1])
    dol_ref[...] = dot(dh_ref[...], wp[...]).astype(BF16)


def attend_back(saved, grads, spare):
    qkv_ref, pt_ref, o_ref = saved
    dol_ref, dl_ref = grads
    score_ref, ds_ref = spare
    low_half = lax.broadcasted_iota(jnp.int32, (TILE, 128), 1) < HEAD_DIM
    items = [(tile, pair) for tile in range(qkv_ref.shape[0] // TILE) for pair in range(HEADS // 2)]

    def spread_probs(index):
        tile, pair = items[index]
        at = slice(tile * TILE, (tile + 1) * TILE)
        here = slice(pair * 128, pair * 128 + 128)
        v = qkv_ref[at, 2 * D + pair * 128 : 2 * D + pair * 128 + 128]
        dol = dol_ref[at, here]
        zero = jnp.zeros_like(v)
        both = jnp.concatenate([jnp.where(low_half, v, zero), jnp.where(low_half, zero, v)], axis=0)
        score_ref[index % SLOTS] = dot_t(both, dol)
        head = tile * HEADS + pair * 2
        dv = dot(pt_ref[head : head + 2].reshape(2 * TILE, TILE), dol)
        dv = jnp.where(low_half, dv[:TILE], dv[TILE:])
        dl_ref[at, 2 * D + pair * 128 : 2 * D + pair * 128 + 128] = dv.astype(BF16)

    lane = jnp.where(lax.broadcasted_iota(jnp.int32, (16, 128), 1) < HEAD_DIM, 0, 1)
    pick = jnp.where(lane == lax.broadcasted_iota(jnp.int32, (16, 128), 0), 1.0, 0.0).astype(BF16)

    def through_softmax(index):
        tile, pair = items[index]
        at = slice(tile * TILE, (tile + 1) * TILE)
        here = slice(pair * 128, pair * 128 + 128)
        means = dot_t(pick, o_ref[at, here] * dol_ref[at, here])
        for side in range(2):
            rows = slice(side * TILE, (side + 1) * TILE)
            for half in blocks(TILE, 128):
                wide = pt_ref[tile * HEADS + pair * 2 + side, :, half].astype(F32)
                piece = score_ref[index % SLOTS, rows, half] - means[side : side + 1, half]
                ds_ref[index % SLOTS, rows, half] = (wide * piece).astype(BF16)

    def to_inputs(index):
        tile, pair = items[index]
        at = slice(tile * TILE, (tile + 1) * TILE)
        here = slice(pair * 128, pair * 128 + 128)
        q = qkv_ref[at, here]
        kt = qkv_ref[at, D + pair * 128 : D + pair * 128 + 128].T
        dk = dot(ds_ref[index % SLOTS], q)
        dl_ref[at, D + pair * 128 : D + pair * 128 + 128] = jnp.where(low_half, dk[:TILE], dk[TILE:]).astype(BF16)
        dqt = [
            dot(
                kt[side * HEAD_DIM : (side + 1) * HEAD_DIM, :],
                ds_ref[index % SLOTS, side * TILE : (side + 1) * TILE, :],
            )
            for side in range(2)
        ]
        dl_ref[at, here] = (jnp.concatenate(dqt, axis=0) * score_scale).astype(BF16).T

    staged(len(items), (spread_probs, through_softmax, to_inputs))


def input_back(h_ref, wq, vec_ref, grads, vg_ref, dx_put):
    dl_ref, keep_ref = grads
    da1 = dot(dl_ref[...], wq[...])
    totals = [jnp.zeros((8, D), F32) for _ in range(2)]
    for at in blocks(h_ref.shape[0], SUB):
        unit, spread = normalise(h_ref[at, :].astype(F32))
        grad = da1[at]
        dx_put(at, keep_ref[at, :] + norm_back(grad, unit, spread, vec_ref[0:1, :]))
        totals = [old + fold(new) for old, new in zip(totals, (grad * unit, grad))]
    add_row(vg_ref, 0, totals[0])
    add_row(vg_ref, 1, totals[1])


def backward_chunk(dy_at, h_ref, weights, vec_ref, saved, grads, spare, vg_ref, dx_put):
    wq, wp, w1, w2 = weights
    qkv_ref, pt_ref, o_ref, h1_ref, gp_ref = saved
    dy_ref, dz_ref, dh_ref, dol_ref, dl_ref, keep_ref = grads
    early = (dy_ref, dz_ref, dh_ref, dol_ref, keep_ref)
    expand_back(dy_at, (wp, w1, w2), vec_ref, (h1_ref, gp_ref), early, vg_ref)
    attend_back((qkv_ref, pt_ref, o_ref), (dol_ref, dl_ref), spare)
    input_back(h_ref, wq, vec_ref, (dl_ref, keep_ref), vg_ref, dx_put)


def pick_halves(first, second, width):
    lane = lax.broadcasted_iota(jnp.int32, first.shape, 1)
    return jnp.where(lane < width, first, second)


ONES = 16


def turn_rows(source, turned):
    for part in range(ROWS // 128):
        here = slice(part * 128, part * 128 + 128)
        turned[0:D, here] = source[here, :].T
        turned[D:, here] = jnp.ones((ONES, 128), BF16)


def put_pack(slab_ref, kind, f, value):
    slab_ref[kind, f // 2, f % 2] = value.astype(BF16).reshape(4, 2, SHARD, D)


def down_grads(dy_s, u_s, turned, slab_ref):
    turn_rows(dy_s, turned)
    made = {}

    def multiply(part):
        made[part] = dot(turned[0:D], u_s[:, part * 2 * D : (part + 1) * 2 * D])

    def pack(part):
        for half in range(2):
            couple = 2 * part + half
            grad = made[part][:, half * D : (half + 1) * D]
            for f in range(4):
                top = grad[f * 96 : f * 96 + 48, :]
                bottom = grad[f * 96 + 48 : f * 96 + 96, :]
                even = pick_halves(top, pltpu.roll(bottom, 192, 1), 192)
                odd = pick_halves(pltpu.roll(top, 192, 1), bottom, 192)
                slab_ref[2, f // 2, f % 2, couple, 0] = even.astype(BF16)
                slab_ref[2, f // 2, f % 2, couple, 1] = odd.astype(BF16)

    staged(2, (multiply, pack))


def up_grads(a2_s, dz_s, turned, slab_ref, vg_ref):
    turn_rows(a2_s, turned)
    made = {}

    def multiply(part):
        made[part] = dot(turned[...], dz_s[:, part * 2 * D : (part + 1) * 2 * D])

    def pack(part):
        for half in range(2):
            f = 2 * part + half
            grad = made[part][:, half * D : (half + 1) * D]
            put_pack(slab_ref, 1, f, grad[0:D])
            vg_ref[7 + f : 8 + f, :] = grad[D : D + 1]

    staged(2, (multiply, pack))


def attention_grads(a1_s, dl_s, o_s, dh_s, turned, slab_ref, vg_ref):
    turn_rows(o_s, turned)
    proj = dot(turned[...], dh_s[...])
    vg_ref[6:7, :] = proj[D : D + 1]
    proj = proj[0:D]
    turn_rows(a1_s, turned)
    both = dot(turned[...], dl_s[:, 0 : 2 * D])
    third = dot(turned[...], dl_s[:, 2 * D : 3 * D])
    first, second = both[0:D, 0:D], both[0:D, D : 2 * D]
    vg_ref[4:5, :] = both[D : D + 1, 0:D]
    put_pack(slab_ref, 0, 0, pick_halves(first, pltpu.roll(proj, 288, 1), 288))
    mixed = pick_halves(pltpu.roll(first, 96, 1), pltpu.roll(second, 96, 1), 96)
    put_pack(slab_ref, 0, 1, pick_halves(mixed, pltpu.roll(proj, 192, 1), 288))
    vg_ref[5:6, :] = third[D : D + 1]
    third = third[0:D]
    mixed = pick_halves(pltpu.roll(second, 192, 1), pltpu.roll(third, 192, 1), 192)
    put_pack(slab_ref, 0, 2, pick_halves(mixed, pltpu.roll(proj, 96, 1), 288))
    put_pack(slab_ref, 0, 3, pick_halves(pltpu.roll(third, 288, 1), proj, 288))


def weight_grads(a1_s, dl_s, o_s, dh_s, a2_s, dz_s, u_s, dy_s, turned, slab_ref, vg_ref):
    down_grads(dy_s, u_s, turned, slab_ref)
    up_grads(a2_s, dz_s, turned, slab_ref, vg_ref)
    attention_grads(a1_s, dl_s, o_s, dh_s, turned, slab_ref, vg_ref)


def rows_block(width, dtype=None):
    return pl.BlockSpec((CHUNK, width), lambda i: (i, 0))


def whole(shape):
    return pl.BlockSpec(shape, lambda i: (0,) * len(shape), pipeline_mode=pl.Buffered(1))


WEIGHT_SPECS = [whole((3 * D, D)), whole((D, D)), whole((D, FF)), whole((D, FF)), whole((16, D))]
BIAS_SPEC = pl.BlockSpec((1, TILE, TILE), lambda i: ((i * PER_STEP) // VIEWS, 0, 0))
PT_SPEC = pl.BlockSpec((PER_STEP * HEADS, TILE, TILE), lambda i: (i, 0, 0))
PARAMS = pltpu.CompilerParams(dimension_semantics=("arbitrary",), vmem_limit_bytes=VMEM_LIMIT)


SPARE = [pltpu.VMEM((SLOTS, 2 * TILE, TILE), F32), pltpu.VMEM((SLOTS, 2 * TILE, TILE), BF16)]


def sequence_start(tile):
    if tile < VIEWS:
        return tile * GLOB_TOK, GLOB_TOK
    group = CROP_GROUP * CROP_TOK
    return VIEWS * GLOB_TOK + (tile - VIEWS) * group, group


def untile(step, source, target):
    per_step = source.shape[0] // TILE
    for turn in range(TILES // per_step):

        @pl.when(step == turn)
        def _():
            for tile in range(per_step):
                start, size = sequence_start(turn * per_step + tile)
                target[start : start + size, :] = source[tile * TILE : tile * TILE + size, :]


def first_forward(rows, bias, weights, vec):
    def kernel(x_ref, bias_ref, wq, wp, w1, w2, vec_ref, out_ref, *rest):
        saved, score_ref = rest[:8], rest[8]

        def finish(at, rows):
            out_ref[at, :] = rows

        forward_chunk(x_ref, bias_ref, (wq, wp, w1, w2), vec_ref, saved, (score_ref,), finish)

    shapes = [
        ((ROWS, D), F32, rows_block(D)),
        ((ROWS, D), BF16, rows_block(D)),
        ((ROWS, 3 * D), BF16, rows_block(3 * D)),
        ((TILES * HEADS, TILE, TILE), BF16, PT_SPEC),
        ((ROWS, D), BF16, rows_block(D)),
        ((ROWS, D), F32, rows_block(D)),
        ((ROWS, D), BF16, rows_block(D)),
        ((ROWS, FF), BF16, rows_block(FF)),
        ((ROWS, FF), BF16, rows_block(FF)),
    ]
    outs = pl.pallas_call(
        kernel,
        grid=(STEPS,),
        in_specs=[rows_block(D), BIAS_SPEC] + WEIGHT_SPECS,
        out_specs=[spec for _, _, spec in shapes],
        out_shape=[jax.ShapeDtypeStruct(shape, dtype) for shape, dtype, _ in shapes],
        scratch_shapes=SPARE[:1],
        compiler_params=PARAMS,
        name="first_forward",
    )(rows, bias, *weights, vec)
    return outs[0], outs[1:]


def row_facts(step, count, per_step):
    row = lax.broadcasted_iota(jnp.int32, (per_step * TILE, 1), 0)
    tile = jnp.zeros_like(row)
    for edge in range(1, per_step):
        tile = tile + jnp.where(row >= edge * TILE, 1, 0)
    local = row - tile * TILE
    tile = tile + step * per_step
    crop = jnp.zeros_like(row)
    for edge in range(1, CROP_GROUP):
        crop = crop + jnp.where(local >= edge * CROP_TOK, 1, 0)
    start = local == crop * CROP_TOK
    crop_id = (tile - VIEWS) * CROP_GROUP + crop
    is_glob = tile < VIEWS
    glob_live = jnp.where(local < GLOB_TOK, 1, 0)
    crop_live = jnp.where(local < CROP_GROUP * CROP_TOK, 1, 0) * jnp.where(crop_id < count, 1, 0)
    live = jnp.where(is_glob, glob_live, crop_live)
    glob_cls = jnp.where(local == 0, tile, -1)
    crop_cls = jnp.where(start, crop_id + VIEWS, -1)
    return live, jnp.where(is_glob, glob_cls, crop_cls)


def second_block(rows, bias, weights, vec, cotangent, returned, count):
    per_step = 1
    chunk, steps = per_step * TILE, TILES // per_step

    def chunk_block(width):
        return pl.BlockSpec((chunk, width), lambda i: (i, 0))

    def kernel(
        count_ref, h_ref, cot_ref, ret_ref, bias_ref, wq, wp, w1, w2, vec_ref,
        act_ref, cls_ref, dx_ref, slab_ref, vg_ref,
        a1_s, qkv_s, pt_s, o_s, h1_s, a2_s, u_s, gp_s, dy_s, dz_s, dh_s, dol_s, dl_s, turned, cls_s, dy_in, keep_s, act_s, wide_s, *spare,
    ):
        step = pl.program_id(0)
        here = pl.ds(pl.multiple_of(step * chunk, chunk), chunk)

        @pl.when(step == 0)
        def _():
            vg_ref[...] = jnp.zeros_like(vg_ref)
            cls_s[...] = jnp.zeros_like(cls_s)

        weights = (wq, wp, w1, w2)
        live, cls_id = row_facts(step, count_ref[0, 0], per_step)
        alive = live.astype(F32)
        spot = lax.broadcasted_iota(jnp.int32, (chunk, CLS_PAD), 1) == cls_id
        spot = jnp.where(spot, 1.0, 0.0).astype(BF16)
        extra = dot(spot, ret_ref[...])
        for at in blocks(chunk, SUB):
            dy_in[at, :] = (cot_ref[at, :].astype(F32) + extra[at]) * alive[at]

        def finish(at, rows):
            rows = rows * alive[at]
            act_s[at, :] = rows

        saved = (a1_s.at[here], qkv_s, pt_s, o_s.at[here], h1_s, a2_s.at[here], u_s.at[here], gp_s)
        forward_chunk(h_ref, bias_ref, weights, vec_ref, saved, spare, finish)
        cls_s[...] += lax.dot_general(
            spot, act_s[...].astype(BF16), (((0,), (0,)), ((), ())), preferred_element_type=F32
        )
        untile(step, act_s, wide_s)
        grads = (dy_s.at[here], dz_s.at[here], dh_s.at[here], dol_s, dl_s.at[here], keep_s)

        def dx_put(at, rows):
            dx_ref[at, :] = rows

        backward_chunk(
            lambda at: dy_in[at, :], h_ref, weights, vec_ref, (qkv_s, pt_s, o_s.at[here], h1_s, gp_s), grads, spare,
            vg_ref, dx_put,
        )

        @pl.when(step == steps - 1)
        def _():
            cls_ref[...] = cls_s[...].astype(BF16)
            act_ref[...] = wide_s[...].astype(BF16)
            weight_grads(a1_s, dl_s, o_s, dh_s, a2_s, dz_s, u_s, dy_s, turned, slab_ref, vg_ref)

    return pl.pallas_call(
        kernel,
        grid=(steps,),
        in_specs=[
            pl.BlockSpec(memory_space=pltpu.SMEM),
            chunk_block(D),
            chunk_block(D),
            whole((CLS_PAD, D)),
            pl.BlockSpec((1, TILE, TILE), lambda i: (i * per_step // VIEWS, 0, 0)),
        ]
        + WEIGHT_SPECS,
        out_specs=[
            whole((TOK_DEV, D)),
            whole((CLS_PAD, D)),
            chunk_block(D),
            whole(SPLIT),
            whole((16, D)),
        ],
        out_shape=[
            jax.ShapeDtypeStruct((TOK_DEV, D), BF16),
            jax.ShapeDtypeStruct((CLS_PAD, D), BF16),
            jax.ShapeDtypeStruct((ROWS, D), F32),
            jax.ShapeDtypeStruct(SPLIT, BF16),
            jax.ShapeDtypeStruct((16, D), F32),
        ],
        scratch_shapes=[
            pltpu.VMEM((ROWS, D), BF16),
            pltpu.VMEM((chunk, 3 * D), BF16),
            pltpu.VMEM((per_step * HEADS, TILE, TILE), BF16),
            pltpu.VMEM((ROWS, D), BF16),
            pltpu.VMEM((chunk, D), F32),
            pltpu.VMEM((ROWS, D), BF16),
            pltpu.VMEM((ROWS, FF), BF16),
            pltpu.VMEM((chunk, FF), BF16),
            pltpu.VMEM((ROWS, D), BF16),
            pltpu.VMEM((ROWS, FF), BF16),
            pltpu.VMEM((ROWS, D), BF16),
            pltpu.VMEM((chunk, D), BF16),
            pltpu.VMEM((ROWS, 3 * D), BF16),
            pltpu.VMEM((D + ONES, ROWS), BF16),
            pltpu.VMEM((CLS_PAD, D), F32),
            pltpu.VMEM((chunk, D), F32),
            pltpu.VMEM((chunk, D), F32),
            pltpu.VMEM((chunk, D), F32),
            pltpu.VMEM((TOK_DEV, D), F32),
        ]
        + SPARE,
        compiler_params=PARAMS,
        name="second_block",
    )(count, rows, cotangent, returned, bias, *weights, vec)


def first_backward(dy, rows, saved, weights, vec):
    def kernel(
        dy_ref, x_ref, a1_hbm, qkv_ref, pt_ref, o_ref, h1_ref, a2_hbm, u_hbm, gp_ref, wq, wp, w1, w2, vec_ref,
        dx_ref, slab_ref, vg_ref,
        a1_s, o_s, a2_s, u_s, dy_s, dz_s, dh_s, dol_s, dl_s, turned, keep_s, dx_s, load_sem, *spare,
    ):
        moves = ((a1_hbm, a1_s), (a2_hbm, a2_s), (u_hbm, u_s))
        loads = [pltpu.make_async_copy(there, mine, load_sem.at[i]) for i, (there, mine) in enumerate(moves)]
        step = pl.program_id(0)
        here = pl.ds(pl.multiple_of(step * CHUNK, CHUNK), CHUNK)

        @pl.when(step == 0)
        def _():
            vg_ref[...] = jnp.zeros_like(vg_ref)
            for load in loads:
                load.start()

        o_s[here] = o_ref[...]
        grads = (dy_s.at[here], dz_s.at[here], dh_s.at[here], dol_s, dl_s.at[here], keep_s)

        def dx_put(at, rows):
            dx_s[at, :] = rows

        backward_chunk(
            lambda at: dy_ref[at, :], x_ref, (wq, wp, w1, w2), vec_ref,
            (qkv_ref, pt_ref, o_ref, h1_ref, gp_ref), grads, spare, vg_ref, dx_put,
        )
        untile(step, dx_s, dx_ref)

        @pl.when(step == STEPS - 1)
        def _():
            for load in loads:
                load.wait()
            weight_grads(a1_s, dl_s, o_s, dh_s, a2_s, dz_s, u_s, dy_s, turned, slab_ref, vg_ref)

    there = pl.BlockSpec(memory_space=pl.ANY)
    return pl.pallas_call(
        kernel,
        grid=(STEPS,),
        in_specs=[
            rows_block(D),
            rows_block(D),
            there,
            rows_block(3 * D),
            PT_SPEC,
            rows_block(D),
            rows_block(D),
            there,
            there,
            rows_block(FF),
        ]
        + WEIGHT_SPECS,
        out_specs=[whole((TOK_DEV, D)), whole(SPLIT), whole((16, D))],
        out_shape=[
            jax.ShapeDtypeStruct((TOK_DEV, D), F32),
            jax.ShapeDtypeStruct(SPLIT, BF16),
            jax.ShapeDtypeStruct((16, D), F32),
        ],
        scratch_shapes=[
            pltpu.VMEM((ROWS, D), BF16),
            pltpu.VMEM((ROWS, D), BF16),
            pltpu.VMEM((ROWS, D), BF16),
            pltpu.VMEM((ROWS, FF), BF16),
            pltpu.VMEM((ROWS, D), BF16),
            pltpu.VMEM((ROWS, FF), BF16),
            pltpu.VMEM((ROWS, D), BF16),
            pltpu.VMEM((CHUNK, D), BF16),
            pltpu.VMEM((ROWS, 3 * D), BF16),
            pltpu.VMEM((D + ONES, ROWS), BF16),
            pltpu.VMEM((CHUNK, D), F32),
            pltpu.VMEM((CHUNK, D), F32),
            pltpu.SemaphoreType.DMA((4,)),
        ]
        + SPARE,
        compiler_params=PARAMS,
        name="first_backward",
    )(dy, rows, *saved, *weights, vec)


def adamw(weight, first_moment, second, gradient, decay_factor, rate):
    new_first = beta_one * first_moment + (1.0 - beta_one) * gradient
    new_second = beta_two * second + (1.0 - beta_two) * gradient * gradient
    first_hat = new_first / (1.0 - beta_one**STEP)
    second_hat = new_second / (1.0 - beta_two**STEP)
    new_weight = weight - rate * (
        first_hat / (jnp.sqrt(second_hat) + adam_epsilon) + decay_factor * weight_decay * weight
    )
    return (new_weight, new_first, new_second)


class Place:
    def __init__(self):
        dp, fsdp = lax.axis_index("dp"), lax.axis_index("fsdp")
        self.dp, self.fsdp = dp, fsdp
        self.z, self.y = dp // 2, dp % 2
        self.x, self.core = fsdp // 2, fsdp % 2

    def along_z(self, step):
        return (lax.rem(self.z + step, 4) * 2 + self.y, self.fsdp)

    def in_plane(self, step):
        x, y = self.plane_spot(step)
        return (self.z * 2 + y, x * 2 + self.core)

    def plane_spot(self, step):
        x = 1 - self.x if step & 1 else self.x
        y = 1 - self.y if step & 2 else self.y
        return x, y

    def along_x(self):
        return (self.dp, (1 - self.x) * 2 + self.core)

    def along_y(self):
        return (self.z * 2 + 1 - self.y, self.fsdp)

    def diagonal(self):
        return (self.z * 2 + 1 - self.y, (1 - self.x) * 2 + self.core)

    def sibling(self):
        return (self.dp, self.x * 2 + 1 - self.core)

    def along_dp(self, step):
        return (lax.rem(self.dp + step, 8), self.fsdp)


def greet(place, along_dp=False):
    barrier = pltpu.get_barrier_semaphore()
    if along_dp:
        others = [place.along_dp(step) for step in range(1, 8)]
        others += [place.in_plane(1), place.in_plane(3), place.sibling()]
    else:
        others = [place.along_z(step) for step in (1, 2, 3)]
        others += [place.in_plane(step) for step in (1, 2, 3)] + [place.sibling()]
    for other in others:
        pl.semaphore_signal(barrier, inc=1, device_id=other, device_id_type=MESH)
    pl.semaphore_wait(barrier, len(others))


def remote(source, target, send_sem, recv_sem, device):
    return pltpu.make_async_remote_copy(
        src_ref=source,
        dst_ref=target,
        send_sem=send_sem,
        recv_sem=recv_sem,
        device_id=device,
        device_id_type=MESH,
    )


class Gather:
    def __init__(self, place, items):
        self.place, self.items = place, items

    def copies(self, index, phase):
        place = self.place
        x, core, z, y = place.x, place.core, place.z, place.y
        buf, out_sem, in_sem, short = self.items[index]
        mine = buf.at[x, core, :, y]
        if phase == 0:
            first, plan = 0, [(buf.at[x, core, z, y], place.along_z(s)) for s in (1, 2, 3)]
        elif phase == 1:
            first, plan = 3, [(mine, place.along_x()), (mine, place.along_y())]
            if short:
                plan.append((mine, place.diagonal()))
        elif phase == 2 and not short:
            first = 5
            plan = [(buf.at[1 - x, core, 0:2, y], place.along_y()), (buf.at[x, core, 2:4, 1 - y], place.along_x())]
        else:
            first, plan = 7, [(buf.at[:, core], place.sibling())]
        return [
            remote(part, part, out_sem.at[first + i], in_sem.at[first + i], other)
            for i, (part, other) in enumerate(plan)
        ]

    def arrivals(self, index, phase):
        place = self.place
        x, core, z, y = place.x, place.core, place.z, place.y
        buf, out_sem, in_sem, short = self.items[index]
        if phase == 0:
            first, spots = 0, [buf.at[x, core, lax.rem(z + 4 - s, 4), y] for s in (1, 2, 3)]
        elif phase == 1:
            first, spots = 3, [buf.at[1 - x, core, :, y], buf.at[x, core, :, 1 - y]]
            if short:
                spots.append(buf.at[1 - x, core, :, 1 - y])
        elif phase == 2 and not short:
            first, spots = 5, [buf.at[1 - x, core, 0:2, 1 - y], buf.at[1 - x, core, 2:4, 1 - y]]
        else:
            first, spots = 7, [buf.at[:, 1 - core]]
        return [
            remote(t, t, out_sem.at[first + i], in_sem.at[first + i], place.sibling()) for i, t in enumerate(spots)
        ]

    def phases(self, index):
        return 3 if self.items[index][3] else 4

    def finish(self, index):
        self.wait(index, self.phases(index) - 1)

    def start(self, index, phase):
        for copy in self.copies(index, phase):
            copy.start()

    def wait(self, index, phase):
        for copy in self.arrivals(index, phase):
            copy.wait_recv()

    def step(self, index, phase):
        self.wait(index, phase)
        self.start(index, phase + 1)

    def drain(self):
        for index in range(len(self.items)):
            for phase in range(self.phases(index)):
                for copy in self.copies(index, phase):
                    copy.wait_send()


def assemble(slabs, kind, targets):
    wq, wp, w1, w2 = targets
    for f in range(4):
        slab = slabs[f // 2, f % 2].reshape(D, D)
        if kind == 0:
            turned = slab.T
            wq[f * 288 : (f + 1) * 288, :] = turned[0:288]
            wp[f * 96 : (f + 1) * 96, :] = turned[288:384]
        elif kind == 1:
            w1[:, f * D : (f + 1) * D] = slab
        else:
            for couple in range(4):
                even = slab[couple * 96 : couple * 96 + 48].astype(F32)
                odd = slab[couple * 96 + 48 : couple * 96 + 96].astype(F32)
                top = pick_halves(even, pltpu.roll(odd, 192, 1), 192)
                bottom = pick_halves(pltpu.roll(even, 192, 1), odd, 192)
                cols = slice(couple * D, (couple + 1) * D)
                w2[f * 96 : f * 96 + 48, cols] = top.astype(BF16)
                w2[f * 96 + 48 : f * 96 + 96, cols] = bottom.astype(BF16)


def late_block(shape, first):
    rest = (0,) * (len(shape) - 1)
    return pl.BlockSpec(shape, lambda i: (jnp.clip(i - first, 0, STEPS - 1), *rest))


def gather_forward(qkv, proj, fc1, fc2, vec, order, cot, tokens, out_cot, bias):
    attend_first, expand_first = 1, 1 + STEPS
    last = 2 * STEPS

    def kernel(
        qkv_ref, proj_ref, fc1_ref, fc2_ref, vec_ref, order_ref, cot_ref, bias_ref, tok_hbm, outc_hbm,
        mid_ref, a1_ref, qkvo_ref, pt_ref, o_ref, h1_ref, a2_ref, u_ref, gp_ref, v0_ref, v1_ref, ret_ref,
        rows_hbm, cot_hbm, wq0_hbm, wp0_hbm, w10_hbm, w20_hbm, wq1_hbm, wp1_hbm, w11_hbm, w21_hbm,
        slabs, vslab, wq, wp, w1, w2, stage, out_cls, in_cls, raw, wide, rows_s, cot_s, h1_s, a2_s, score_s,
        send, recv, vsend, vrecv, csend, crecv, rsem, wsem,
    ):
        step = pl.program_id(0)
        place = Place()
        x, core, z, y = place.x, place.core, place.z, place.y
        items = [(slabs.at[c], send.at[c], recv.at[c], c == 0) for c in range(2 * PACKS)]
        items.insert(0, (vslab, vsend, vrecv, True))
        gather = Gather(place, items)
        loads = [
            pltpu.make_async_copy(tok_hbm.at[0, 0], raw.at[0], rsem.at[0]),
            pltpu.make_async_copy(outc_hbm.at[0, 0], raw.at[1], rsem.at[1]),
        ]
        stores = [
            pltpu.make_async_copy(rows_s, rows_hbm, rsem.at[2]),
            pltpu.make_async_copy(cot_s, cot_hbm, rsem.at[3]),
        ]
        weights = (wq, wp, w1, w2)
        keeps = [
            [
                pltpu.make_async_copy(mine.at[block], there, wsem.at[block, i])
                for i, (mine, there) in enumerate(zip(weights, theirs))
            ]
            for block, theirs in enumerate(
                ((wq0_hbm, wp0_hbm, w10_hbm, w20_hbm), (wq1_hbm, wp1_hbm, w11_hbm, w21_hbm))
            )
        ]
        cls = [
            remote(out_cls.at[s], in_cls.at[s - 1], csend.at[s - 1], crecv.at[s - 1], place.along_dp(s))
            for s in range(1, 8)
        ]

        def pack(block):
            stage[0, :, 0:288] = qkv_ref[block]
            stage[1, :, 0:96] = proj_ref[block]
            first = pick_halves(stage[0], pltpu.roll(stage[1], 288, 1), 288).astype(BF16)
            slabs[block * PACKS, x, core, z, y] = first
            slabs[block * PACKS + 1, x, core, z, y] = fc1_ref[block].astype(BF16)
            turned = fc2_ref[block].T
            stage[0, :, 0:192] = turned[0:48]
            stage[1, :, 0:192] = turned[48:96]
            third = pick_halves(stage[0], pltpu.roll(stage[1], 192, 1), 192).astype(BF16)
            slabs[block * PACKS + 2, x, core, z, y] = third

        def tile_rows(source, target):
            loads[source].wait()
            wide[:TOK_DEV] = raw[source].astype(F32)
            for tile in range(TILES):
                first, _ = sequence_start(tile)
                target[tile * TILE : (tile + 1) * TILE, :] = wide[first : first + TILE, :].astype(BF16)
            stores[source].start()

        def land(index):
            gather.finish(index)
            block, kind = (index - 1) // PACKS, (index - 1) % PACKS
            assemble(slabs.at[index - 1], kind, [w.at[block] for w in weights])
            for i in ((0, 1), (2,), (3,))[kind]:
                keeps[block][i].start()

        @pl.when(step == 0)
        def _():
            for load in loads:
                load.start()
            pack(0)
            stage[0, :, 0:128] = jnp.zeros((SHARD, 128), F32)
            stage[1, :, 0:128] = jnp.zeros((SHARD, 128), F32)
            for i in range(3):
                stage[0, i : i + 1, 0:SHARD] = vec_ref[i, 0:1]
                stage[0, 3 + i : 4 + i, 0:SHARD] = vec_ref[i, 1:2]
            stage[1, :, 0:SHARD] = stage[0, :, 0:128].T[0:SHARD]
            vslab[x, core, z, y] = stage[1, :, 0:128].astype(BF16)
            greet(place, along_dp=True)
            gather.start(0, 0)
            gather.start(1, 0)
            pack(1)
            spots = lax.broadcasted_iota(jnp.int32, (CLS_PAD, CLS_DEV), 0)
            wanted = order_ref[...]
            for s in range(8):
                dest = lax.rem(place.dp + s, 8)
                hit = jnp.logical_and(wanted == spots + dest * CLS_DEV, spots < CLS_DEV)
                hit = jnp.where(hit, 1.0, 0.0).astype(BF16)
                out_cls[s] = dot(hit, cot_ref[0, 0]).astype(BF16)
            gather.step(0, 0)
            gather.step(1, 0)
            gather.start(2, 0)
            gather.start(3, 0)
            v0_ref[...] = jnp.zeros_like(v0_ref)
            v1_ref[...] = jnp.zeros_like(v1_ref)
            wide[TOK_DEV:] = jnp.zeros((WIDE - TOK_DEV, D), F32)
            tile_rows(0, rows_s)
            for at in blocks(ROWS, SUB):
                h1_s[at, :] = normalise(rows_s[at, :].astype(F32))[0]
            gather.step(0, 1)
            gather.step(1, 1)
            gather.step(2, 0)
            gather.step(3, 0)
            for index in range(PACKS + 1, 2 * PACKS + 1):
                gather.start(index, 0)
            tile_rows(1, cot_s)
            gather.wait(0, 2)
            for f in range(4):
                rows = vslab[f // 2, f % 2].reshape(D, 128).astype(F32).T
                for block, v_ref in enumerate((v0_ref, v1_ref)):
                    v_ref[3 * f : 3 * f + 3, :] = rows[block * 3 : block * 3 + 3, :]
            land(1)

        def at_step(turn, *actions):
            @pl.when(step == turn)
            def _():
                for action, *args in actions:
                    action(*args)

        at_step(attend_first + 1, (gather.step, 2, 1), (gather.step, 3, 1), (gather.step, 4, 0))
        at_step(attend_first + 2, (gather.step, 5, 0))
        at_step(attend_first + 3, (gather.step, 2, 2), (gather.step, 3, 2), (gather.step, 4, 1), (gather.step, 6, 0))

        @pl.when(jnp.logical_and(step >= attend_first, step < expand_first))
        def _():
            here = pl.ds(pl.multiple_of((step - attend_first) * CHUNK, CHUNK), CHUNK)

            def put_mid(at, h1, a2):
                h1_ref[at, :] = h1
                a2_ref[at, :] = a2
                h1_s.at[here][at, :] = h1
                a2_s.at[here][at, :] = a2

            saved = (a1_ref, qkvo_ref, pt_ref, o_ref)
            attend_chunk(
                rows_s.at[here], bias_ref, (wq.at[0], wp.at[0]), v0_ref, saved, score_s, put_mid, h1_s.at[here]
            )

        @pl.when(step == expand_first)
        def _():
            for copy in cls:
                copy.start()
            land(2)
            land(3)
            gather.step(5, 1)

        at_step(expand_first + 1, (gather.step, 4, 2), (gather.step, 6, 1))
        at_step(expand_first + 2, (gather.step, 5, 2), (gather.step, 6, 2))
        at_step(expand_first + 3, (land, 4), (land, 5))

        @pl.when(step >= expand_first)
        def _():
            here = pl.ds(pl.multiple_of((step - expand_first) * CHUNK, CHUNK), CHUNK)

            def finish(at, rows):
                mid_ref[at, :] = rows

            expand_chunk(h1_s.at[here], a2_s.at[here], (w1.at[0], w2.at[0]), v0_ref, (u_ref, gp_ref), finish)

        @pl.when(step == last)
        def _():
            for copy in cls:
                copy.wait_recv()
            total = out_cls[0].astype(F32)
            for s in range(7):
                total = total + in_cls[s].astype(F32)
            ret_ref[...] = total.astype(BF16)
            land(6)
            for copy in cls:
                copy.wait_send()
            gather.drain()
            for store in stores + keeps[0] + keeps[1]:
                store.wait()

    vmem = pl.BlockSpec(memory_space=pltpu.VMEM)
    there = pl.BlockSpec(memory_space=pl.ANY)
    early = [
        ((ROWS, D), BF16, CHUNK),
        ((ROWS, 3 * D), BF16, CHUNK),
        ((TILES * HEADS, TILE, TILE), BF16, PER_STEP * HEADS),
        ((ROWS, D), BF16, CHUNK),
        ((ROWS, D), F32, CHUNK),
        ((ROWS, D), BF16, CHUNK),
    ]
    late = [((ROWS, FF), BF16, CHUNK), ((ROWS, FF), BF16, CHUNK)]
    shapes = [((ROWS, D), F32, late_block((CHUNK, D), expand_first))]
    shapes += [(shape, dtype, late_block((size, *shape[1:]), attend_first)) for shape, dtype, size in early]
    shapes += [(shape, dtype, late_block((size, *shape[1:]), expand_first)) for shape, dtype, size in late]
    shapes += [((16, D), F32, whole((16, D)))] * 2 + [((CLS_PAD, D), BF16, whole((CLS_PAD, D)))]
    forms = ((3 * D, D), (D, D), (D, FF), (D, FF))
    shapes += [((ROWS, D), BF16, there)] * 2 + [(form, BF16, there) for form in forms * 2]
    outs = pl.pallas_call(
        kernel,
        grid=(last + 1,),
        in_specs=[whole(a.shape) for a in (qkv, proj, fc1, fc2, vec, order, cot)]
        + [
            pl.BlockSpec(
                (1, TILE, TILE),
                lambda i: ((jnp.clip(i - attend_first, 0, STEPS - 1) * PER_STEP) // VIEWS, 0, 0),
            ),
            there,
            there,
        ],
        out_specs=[spec for _, _, spec in shapes],
        out_shape=[jax.ShapeDtypeStruct(shape, dtype) for shape, dtype, _ in shapes],
        scratch_shapes=[
            pltpu.VMEM((2 * PACKS, *GATHERED), BF16),
            pltpu.VMEM((2, 2, 4, 2, SHARD, 128), BF16),
            *[pltpu.VMEM((2, *form), BF16) for form in forms],
            pltpu.VMEM((2, SHARD, D), F32),
            pltpu.VMEM((8, CLS_PAD, D), BF16),
            pltpu.VMEM((7, CLS_PAD, D), BF16),
            pltpu.VMEM((2, TOK_DEV, D), BF16),
            pltpu.VMEM((WIDE, D), F32),
            pltpu.VMEM((ROWS, D), BF16),
            pltpu.VMEM((ROWS, D), BF16),
            pltpu.VMEM((ROWS, D), F32),
            pltpu.VMEM((ROWS, D), BF16),
            SPARE[0],
            pltpu.SemaphoreType.DMA((2 * PACKS, 8)),
            pltpu.SemaphoreType.DMA((2 * PACKS, 8)),
            pltpu.SemaphoreType.DMA((8,)),
            pltpu.SemaphoreType.DMA((8,)),
            pltpu.SemaphoreType.DMA((7,)),
            pltpu.SemaphoreType.DMA((7,)),
            pltpu.SemaphoreType.DMA((4,)),
            pltpu.SemaphoreType.DMA((2, 4)),
        ],
        compiler_params=pltpu.CompilerParams(
            dimension_semantics=("arbitrary",), collective_id=0, has_side_effects=True, vmem_limit_bytes=VMEM_LIMIT
        ),
        name="gather_forward",
    )(qkv, proj, fc1, fc2, vec, order, cot, bias, tokens, out_cot)
    middle, saved, vecs, returned = outs[0], outs[1:9], outs[9:11], outs[11]
    return middle, saved, vecs, returned, outs[12], outs[13], outs[14:18], outs[18:22]


class Scatter:
    def __init__(self, place, source, sum1, in1, sum2, in2, in3, send, recv):
        self.place, self.source = place, source
        self.sum1, self.in1, self.sum2, self.in2, self.in3 = sum1, in1, sum2, in2, in3
        self.send, self.recv = send, recv

    def copies(self, c, phase):
        place, send, recv = self.place, self.send, self.recv
        if phase == 0:
            mine = self.source.at[c, :, 1 - place.core]
            return [remote(mine, self.in1.at[c], send.at[c, 0], recv.at[c, 0], place.sibling())]
        if phase == 1:
            out = []
            for s in (1, 2, 3):
                px, py = place.plane_spot(s)
                mine = self.sum1.at[c, px, :, py]
                out.append(remote(mine, self.in2.at[c, s - 1], send.at[c, s], recv.at[c, s], place.in_plane(s)))
            return out
        out = []
        for s in (1, 2, 3):
            mine = self.sum2.at[c, lax.rem(place.z + s, 4)]
            out.append(remote(mine, self.in3.at[c, s - 1], send.at[c, 3 + s], recv.at[c, 3 + s], place.along_z(s)))
        return out

    def start(self, c, phase):
        for copy in self.copies(c, phase):
            copy.start()

    def wait(self, c, phase):
        for copy in self.copies(c, phase):
            copy.wait_recv()

    def plane(self, c):
        self.wait(c, 0)
        for px in range(2):
            total = self.source[c, px, self.place.core].astype(F32) + self.in1[c, px].astype(F32)
            self.sum1[c, px] = total.astype(BF16)
        self.start(c, 1)

    def line(self, c):
        self.wait(c, 1)
        total = self.sum1[c, self.place.x, :, self.place.y].astype(F32)
        for s in range(3):
            total = total + self.in2[c, s].astype(F32)
        self.sum2[c] = total.astype(BF16)
        self.start(c, 2)

    def total(self, c):
        self.wait(c, 2)
        total = self.sum2[c, self.place.z].astype(F32)
        for s in range(3):
            total = total + self.in3[c, s].astype(F32)
        return total

    def drain(self, kinds):
        for c in range(kinds):
            for phase in range(3):
                for copy in self.copies(c, phase):
                    copy.wait_send()


SCATTER_SCRATCH = [
    pltpu.VMEM((PACKS, 2, 4, 2, SHARD, D), BF16),
    pltpu.VMEM((PACKS, 2, 4, 2, SHARD, D), BF16),
    pltpu.VMEM((PACKS, 4, SHARD, D), BF16),
    pltpu.VMEM((PACKS, 3, 4, SHARD, D), BF16),
    pltpu.VMEM((PACKS, 3, SHARD, D), BF16),
    pltpu.SemaphoreType.DMA((PACKS, 7)),
    pltpu.SemaphoreType.DMA((PACKS, 7)),
]


def backward_scatter(dy, rows, saved, weights, vec, other, vg_other, cls_rows):
    middle, attend_first = STEPS, STEPS + 1
    turn_back, input_first = 2 * STEPS + 1, 2 * STEPS + 2
    last = 3 * STEPS + 1

    def kernel(
        dy_ref, x_ref, a1_hbm, qkv_ref, pt_ref, o_ref, h1_ref, a2_hbm, u_hbm, gp_ref, wq, wp, w1, w2, vec_ref,
        other_ref, vhi_ref, cls_ref,
        dx_ref, low_ref, high_ref, vsum_ref, cls_out,
        a2_s, u_s, dy_s, dz_s, dh_s, dol_s, turned, keep_s, dx_s, slab_s, vg_s, load_sem, score_s, ds_s, *refs,
    ):
        high_refs, low_refs, (vin, vacc, cls_all, vsend, vrecv, csend, crecv) = refs[0:7], refs[7:14], refs[14:]
        step = pl.program_id(0)
        place = Place()
        high = Scatter(place, other_ref, *high_refs)
        low = Scatter(place, slab_s, *low_refs)
        o_s, a1_s, dl_s = u_s.at[:, 0:D], u_s.at[:, D : 2 * D], dz_s.at[:, 0 : 3 * D]
        moves = ((a2_hbm, a2_s), (u_hbm, u_s), (a1_hbm, a1_s))
        loads = [pltpu.make_async_copy(there, mine, load_sem.at[i]) for i, (there, mine) in enumerate(moves)]
        cls = [
            remote(cls_ref, cls_all.at[place.dp], csend.at[s - 1], crecv.at[s - 1], place.along_dp(s))
            for s in range(1, 8)
        ]
        vec = [remote(vacc.at[0], vin.at[0], vsend.at[0], vrecv.at[0], place.sibling())]
        vec += [
            remote(vacc.at[1], vin.at[s], vsend.at[s], vrecv.at[s], place.in_plane(s)) for s in (1, 2, 3)
        ]
        vec += [
            remote(vacc.at[2], vin.at[3 + s], vsend.at[3 + s], vrecv.at[3 + s], place.along_z(s)) for s in (1, 2, 3)
        ]

        def at_step(turn, *actions):
            @pl.when(step == turn)
            def _():
                for action, *args in actions:
                    action(*args)

        @pl.when(step == 0)
        def _():
            vg_s[...] = jnp.zeros_like(vg_s)
            loads[0].start()
            loads[1].start()
            greet(place, along_dp=True)
            for c in range(PACKS):
                high.start(c, 0)
            cls_all[place.dp] = cls_ref[...]
            for copy in cls:
                copy.start()

        at_step(2, (high.plane, 2), (high.plane, 1), (high.plane, 0))

        @pl.when(step < middle)
        def _():
            here = pl.ds(pl.multiple_of(step * CHUNK, CHUNK), CHUNK)
            grads = (dy_s.at[here], dz_s.at[here], dh_s.at[here], dol_s.at[here], keep_s.at[here])
            expand_back(lambda at: dy_ref[at, :], (wp, w1, w2), vec_ref, (h1_ref, gp_ref), grads, vg_s)

        @pl.when(step == middle)
        def _():
            loads[0].wait()
            loads[1].wait()
            down_grads(dy_s, u_s, turned, slab_s)
            low.start(2, 0)
            loads[2].start()
            up_grads(a2_s, dz_s, turned, slab_s, vg_s)
            low.start(1, 0)

        at_step(attend_first, (high.line, 2))
        at_step(attend_first + 1, (high.line, 1), (low.plane, 2))
        at_step(attend_first + 2, (low.plane, 1))
        at_step(attend_first + 3, (high.line, 0))

        @pl.when(jnp.logical_and(step >= attend_first, step < turn_back))
        def _():
            turn = step - attend_first
            here = pl.ds(pl.multiple_of(turn * CHUNK, CHUNK), CHUNK)

            o_s.at[here][...] = o_ref[...]
            attend_back((qkv_ref, pt_ref, o_ref), (dol_s.at[here], dl_s.at[here]), (score_s, ds_s))

        @pl.when(step == turn_back)
        def _():
            loads[2].wait()
            attention_grads(a1_s, dl_s, o_s, dh_s, turned, slab_s, vg_s)
            low.start(0, 0)

        at_step(input_first + 1, (low.line, 2))
        at_step(input_first + 3, (low.plane, 0))

        @pl.when(step >= input_first)
        def _():
            turn = step - input_first
            here = pl.ds(pl.multiple_of(turn * CHUNK, CHUNK), CHUNK)

            def dx_put(at, rows):
                dx_s[at, :] = rows

            input_back(x_ref, wq, vec_ref, (dl_s.at[here], keep_s.at[here]), vg_s, dx_put)
            untile(turn, dx_s, dx_ref)

        @pl.when(step == last)
        def _():
            vacc[0, 0:16] = vg_s[...]
            vacc[0, 16:32] = vhi_ref[...]
            vec[0].start()
            low.line(1)
            for c in range(PACKS):
                high_ref[c] = high.total(c)
            vec[0].wait_recv()
            vacc[1] = vacc[0] + vin[0]
            for copy in vec[1:4]:
                copy.start()
            low_ref[2] = low.total(2)
            for copy in cls:
                copy.wait_recv()
            cls_out[...] = cls_all[...]
            for copy in vec[1:4]:
                copy.wait_recv()
            vacc[2] = vacc[1] + vin[1] + vin[2] + vin[3]
            for copy in vec[4:7]:
                copy.start()
            low.line(0)
            low_ref[1] = low.total(1)
            for copy in vec[4:7]:
                copy.wait_recv()
            vsum_ref[...] = vacc[2] + vin[4] + vin[5] + vin[6]
            low_ref[0] = low.total(0)
            for copy in cls + vec:
                copy.wait_send()
            high.drain(PACKS)
            low.drain(PACKS)

    there = pl.BlockSpec(memory_space=pl.ANY)

    def early(width):
        return late_block((CHUNK, width), 0)

    def late(width):
        return late_block((CHUNK, width), attend_first)

    out_shapes = [
        ((TOK_DEV, D), F32),
        ((PACKS, SHARD, D), F32),
        ((PACKS, SHARD, D), F32),
        ((32, D), F32),
        ((8, CLS_PAD, D), BF16),
    ]
    return pl.pallas_call(
        kernel,
        grid=(last + 1,),
        in_specs=[
            early(D),
            late_block((CHUNK, D), input_first),
            there,
            late(3 * D),
            late_block((PER_STEP * HEADS, TILE, TILE), attend_first),
            late(D),
            early(D),
            there,
            there,
            early(FF),
        ]
        + WEIGHT_SPECS
        + [whole(SPLIT), whole((16, D)), whole((CLS_PAD, D))],
        out_specs=[whole(shape) for shape, _ in out_shapes],
        out_shape=[jax.ShapeDtypeStruct(shape, dtype) for shape, dtype in out_shapes],
        scratch_shapes=[
            pltpu.VMEM((ROWS, D), BF16),
            pltpu.VMEM((ROWS, FF), BF16),
            pltpu.VMEM((ROWS, D), BF16),
            pltpu.VMEM((ROWS, FF), BF16),
            pltpu.VMEM((ROWS, D), BF16),
            pltpu.VMEM((ROWS, D), BF16),
            pltpu.VMEM((D + ONES, ROWS), BF16),
            pltpu.VMEM((ROWS, D), F32),
            pltpu.VMEM((CHUNK, D), F32),
            pltpu.VMEM(SPLIT, BF16),
            pltpu.VMEM((16, D), F32),
            pltpu.SemaphoreType.DMA((4,)),
        ]
        + SPARE
        + SCATTER_SCRATCH * 2
        + [
            pltpu.VMEM((7, 32, D), F32),
            pltpu.VMEM((3, 32, D), F32),
            pltpu.VMEM((8, CLS_PAD, D), BF16),
            pltpu.SemaphoreType.DMA((7,)),
            pltpu.SemaphoreType.DMA((7,)),
            pltpu.SemaphoreType.DMA((7,)),
            pltpu.SemaphoreType.DMA((7,)),
        ],
        compiler_params=pltpu.CompilerParams(
            dimension_semantics=("arbitrary",), collective_id=1, has_side_effects=True, vmem_limit_bytes=VMEM_LIMIT
        ),
        name="backward_scatter",
    )(dy, rows, *saved, *weights, vec, other, vg_other, cls_rows)


def apply_updates(low, high, vec_sum, cls_all, order, state, vec_state):
    def kernel(low_ref, high_ref, vsum_ref, cls_ref, order_ref, *rest):
        state, vecs, outs, vec_outs = rest[0:12], rest[12:15], rest[15:27], rest[27:30]
        regroup_ref = rest[30]

        def update(kind, block, grad):
            w_ref, m_ref, s_ref = state[kind], state[4 + kind], state[8 + kind]
            new = adamw(w_ref[block], m_ref[block], s_ref[block], grad, 1.0, step_rate)
            for slot in range(3):
                outs[slot * 4 + kind][block] = new[slot]

        for block, grad_ref in enumerate((low_ref, high_ref)):
            total = grad_ref[0]
            update(0, block, total[:, 0:288])
            update(1, block, pltpu.roll(total, 96, 1)[:, 0:96])
            update(2, block, grad_ref[1])
            total = grad_ref[2]
            both = jnp.concatenate([total[:, 0:192], pltpu.roll(total, 192, 1)[:, 0:192]], axis=0)
            update(3, block, both.T)
        dp, fsdp = lax.axis_index("dp"), lax.axis_index("fsdp")
        mine = pltpu.roll(vsum_ref[...], lax.rem(D - dp * SHARD, D), 1)
        mine = pltpu.roll(mine, lax.rem(32 - 3 * fsdp, 32), 0)
        for column in range(3):
            grad = jnp.concatenate([mine[16 * b + column : 16 * b + column + 1, 0:SHARD] for b in range(2)], axis=0)
            new = adamw(vecs[0][column], vecs[1][column], vecs[2][column], grad, 0.0, vector_rate)
            for slot in range(3):
                vec_outs[slot][column] = new[slot]
        spots = lax.broadcasted_iota(jnp.int32, (8 * CLS_PAD, CLS_DEV), 0)
        code = (spots // CLS_PAD) * CLS_DEV + spots % CLS_PAD
        hit = jnp.logical_and(order_ref[...] == code, spots % CLS_PAD < CLS_DEV)
        hit = jnp.where(hit, 1.0, 0.0).astype(BF16)
        regrouped = lax.dot_general(
            hit, cls_ref[...].reshape(8 * CLS_PAD, D), (((0,), (0,)), ((), ())), preferred_element_type=F32
        )
        regroup_ref[0, 0] = regrouped.astype(BF16)

    out_shape = [jax.ShapeDtypeStruct(a.shape, F32) for a in (*state, *vec_state)]
    out_shape.append(jax.ShapeDtypeStruct((1, 1, CLS_DEV, D), BF16))
    vmem = pl.BlockSpec(memory_space=pltpu.VMEM)
    return pl.pallas_call(
        kernel,
        out_shape=out_shape,
        in_specs=[vmem] * 20,
        out_specs=[vmem] * 16,
        compiler_params=pltpu.CompilerParams(vmem_limit_bytes=VMEM_LIMIT),
        name="apply_updates",
    )(low, high, vec_sum, cls_all, order, *state, *vec_state)


def tile_rows(rows):
    edge = VIEWS * GLOB_TOK
    glob = rows[:edge].reshape(VIEWS, GLOB_TOK, D)
    crop = rows[edge:].reshape(GROUPS, CROP_GROUP * CROP_TOK, D)
    glob = jnp.pad(glob, ((0, 0), (0, TILE - GLOB_TOK), (0, 0)))
    crop = jnp.pad(crop, ((0, 0), (0, TILE - CROP_GROUP * CROP_TOK), (0, 0)))
    return jnp.concatenate([glob, crop], axis=0).reshape(ROWS, D)


def mask_bias():
    row = np.arange(TILE)
    glob = row // GLOB_TOK
    crop = np.minimum(row // CROP_TOK, CROP_GROUP)
    same = np.stack([group[:, None] == group[None, :] for group in (glob, crop)])
    return np.where(same, 0.0, -1e30).astype(np.float32)


def local_fast(
    tokens, focal_count, cls_order, out_cotangent, cls_cotangent,
    qkv_weight, proj_weight, fc1_weight, fc2_weight, vec_params,
    qkv_first, proj_first, fc1_first, fc2_first, vec_first,
    qkv_second, proj_second, fc1_second, fc2_second, vec_second,
):
    def turn(narrow):
        return narrow.transpose(2, 0, 1)

    bias = jnp.asarray(mask_bias())
    middle, saved, vec, returned, rows, cotangent, lower, upper = gather_forward(
        qkv_weight, proj_weight, fc1_weight, fc2_weight, turn(vec_params),
        cls_order, cls_cotangent, tokens, out_cotangent, bias,
    )
    shown, cls_rows, middle_grad, slab_hi, vg_hi = second_block(
        middle, bias, upper, vec[1], cotangent, returned, focal_count
    )
    input_grad, low, high, vec_sum, cls_all = backward_scatter(
        middle_grad, rows, saved, lower, vec[0], slab_hi, vg_hi, cls_rows
    )
    state = (
        qkv_weight, proj_weight, fc1_weight, fc2_weight,
        qkv_first, proj_first, fc1_first, fc2_first,
        qkv_second, proj_second, fc1_second, fc2_second,
    )
    vec_state = (turn(vec_params), turn(vec_first), turn(vec_second))
    out = apply_updates(low, high, vec_sum, cls_all, cls_order, state, vec_state)
    return (
        shown[None, None],
        out[15],
        input_grad[None, None],
        *out[0:4], out[12].transpose(1, 2, 0),
        *out[4:8], out[13].transpose(1, 2, 0),
        *out[8:12], out[14].transpose(1, 2, 0),
    )


def local_any(
    tokens, focal_count, cls_order, out_cotangent, cls_cotangent,
    qkv_weight, proj_weight, fc1_weight, fc2_weight, vec_params,
    qkv_first, proj_first, fc1_first, fc2_first, vec_first,
    qkv_second, proj_second, fc1_second, fc2_second, vec_second,
):
    def gather(shard):
        wide = lax.all_gather(shard.astype(BF16), "fsdp", axis=2, tiled=True)
        return lax.all_gather(wide, "dp", axis=1, tiled=True)

    params = (qkv_weight, proj_weight, fc1_weight, fc2_weight, vec_params)
    qkv, proj, fc1, fc2, vectors = (gather(param) for param in params)
    blocks = [(qkv[b].T, proj[b].T, fc1[b], fc2[b].T) for b in range(2)]
    vec = jnp.pad(vectors.astype(F32).transpose(0, 2, 1), ((0, 0), (0, 4), (0, 0)))
    dp, fsdp = lax.axis_index("dp"), lax.axis_index("fsdp")
    total_cls = lax.axis_size("dp") * CLS_DEV
    picker = (cls_order[0][:, None] == jnp.arange(total_cls, dtype=jnp.int32)[None, :]).astype(BF16)
    spread = lax.dot_general(
        picker, cls_cotangent[0, 0], (((0,), (0,)), ((), ())), preferred_element_type=F32
    )
    returned = lax.psum_scatter(spread, "dp", scatter_dimension=0, tiled=True).astype(BF16)
    returned = jnp.pad(returned, ((0, CLS_PAD - CLS_DEV), (0, 0)))
    bias = jnp.asarray(mask_bias())
    rows = tile_rows(tokens[0, 0])
    middle, saved = first_forward(rows, bias, blocks[0], vec[0])
    shown, cls_rows, middle_grad, slab_hi, vg_hi = second_block(
        middle, bias, blocks[1], vec[1], tile_rows(out_cotangent[0, 0]), returned, focal_count
    )
    input_grad, slab_lo, vg_lo = first_backward(middle_grad, rows, saved, blocks[0], vec[0])
    slabs, vg = (slab_lo, slab_hi), (vg_lo, vg_hi)
    pooled = lax.all_gather(cls_rows[:CLS_DEV], "dp", axis=0, tiled=True)
    regrouped = jnp.dot(picker, pooled, preferred_element_type=F32).astype(BF16)

    def scatter(full):
        rows = lax.psum_scatter(full, "dp", scatter_dimension=1, tiled=True)
        return lax.psum_scatter(rows, "fsdp", scatter_dimension=2, tiled=True)

    packs = jnp.stack(slabs).reshape(2, PACKS, 4, D, D).astype(F32)
    qkv_full = packs[:, 0, :, :, 0:288].transpose(0, 2, 1, 3).reshape(2, D, 3 * D)
    proj_full = packs[:, 0, :, :, 288:384].transpose(0, 2, 1, 3).reshape(2, D, D)
    fc1_full = packs[:, 1].transpose(0, 2, 1, 3).reshape(2, D, FF)
    turned = packs[:, 2].reshape(2, 4, 8, SHARD, 2, 192)
    fc2_full = turned.transpose(0, 2, 5, 1, 4, 3).reshape(2, FF, D)
    vec_full = jnp.stack(vg)[:, :12].transpose(0, 2, 1)
    owned = [scatter(full) for full in (qkv_full, proj_full, fc1_full, fc2_full, vec_full)]
    firsts = (qkv_first, proj_first, fc1_first, fc2_first, vec_first)
    seconds = (qkv_second, proj_second, fc1_second, fc2_second, vec_second)
    flags = (1.0, 1.0, 1.0, 1.0, 0.0)
    rates = (step_rate,) * 4 + (vector_rate,)
    new = [adamw(*args) for args in zip(params, firsts, seconds, owned, flags, rates)]
    return (
        shown[None, None],
        regrouped[None, None],
        input_grad[None, None],
        *(item[0] for item in new),
        *(item[1] for item in new),
        *(item[2] for item in new),
    )


def solution(mesh):
    sizes = dict(mesh.shape)
    local = local_fast if (sizes["dp"], sizes["fsdp"]) == (8, 4) else local_any
    weight = P(None, "dp", "fsdp")
    rows = P("dp", "fsdp", None, None)
    return jax.shard_map(
        local,
        mesh=mesh,
        in_specs=(rows, P("dp", "fsdp"), P("fsdp", "dp"), rows, rows) + (weight,) * 15,
        out_specs=(rows, rows, rows) + (weight,) * 15,
        check_vma=False,
    )
```

time: 1470 us -> 196 us (0.13)
  waiting for transfers between devices: 534 us -> 0 us
  blocking collectives: 304 us -> 0 us
  local copies, waits for them, and re-layouts: 269 us -> 1.41 us
  matrix products: 267 us -> 0 us
  Pallas kernels: 0 us -> 194 us
  other arithmetic: 65.3 us -> 0 us
  between operations: 18 us -> 1.34 us
    reduce_scatter x10 -> x0, waiting for transfers between devices: 320 us -> none  [the longest x2 139 us: scatter_gradients(): lax.psum_scatter(gradients[2], 'dp', scatter_dimension=0, tiled=True)]
    all_gather x17 -> x0, blocking collectives: 294 us -> none  [the longest x6 197 us: gather_forward(): lax.all_gather(as_sent(column_full), 'dp', axis=0, tiled=True)]
    dot_general x48 -> x0, matrix products: 257 us -> none  [the longest x8 59.9 us: times_transpose(): lax.dot_general(left_side, right_side, (((1,), (1,)), ((), ())), preferre...]
    unnamed x32 -> x0, waiting for transfers between devices: 213 us -> none
    pallas_call x0 -> x4, Pallas kernels: none -> 194 us  [the longest x1 65 us: backward_scatter(): pl.pallas_call(kernel, grid=(last + 1,), in_specs=[early(D), late_block((...]
    reshape x56 -> x0, local copies, waits for them, and re-layouts: 149 us -> none  [the longest x16 61.7 us: over_groups(): second_out.reshape(CROPS * CROP_TOK, -1)]
    unnamed x290 -> x3, local copies, waits for them, and re-layouts: 46 us -> 1.41 us
    reduce_sum x24 -> x0, other arithmetic: 29.6 us -> none  [the longest x6 9.05 us: block_backward(): jnp.sum(value_grad, axis=0)]
  transfers between devices with their start and end apart: 23 -> 0, of which waited for: 15 -> 0; matrix products, arithmetic and copies ran while one was open for 36% -> 0% of each run, Pallas kernels for 0% -> 0%
where the time goes in v1:
time: 196 us
  Pallas kernels  194 us (99%)
    pallas_call x1, Pallas kernels, backward_scatter(): pl.pallas_call(kernel, grid=(last + 1,), in_specs=[early(D), late_block((...  65 us
    pallas_call x1, Pallas kernels, second_block(): pl.pallas_call(kernel, grid=(steps,), in_specs=[pl.BlockSpec(memory_space...  63.6 us
    pallas_call x1, Pallas kernels, gather_forward(): pl.pallas_call(kernel, grid=(last + 1,), in_specs=[whole(a.shape) for a i...  61.5 us

profile of v1, /device:TPU:0, one launch (start us, length us, event | category | flops | bytes accessed | tf_op | source)
XLA Modules:
  0.0 196.3 jit_solution(15001648637070164176)
XLA Ops:
  1.3 61.5 %gather_forward.1 = (f32[1664,384]{1,0:T(8,128)}, bf16[1664,384]{1,0:T(8,128)(2,1)}, bf16[1664,1152]{1,0:T(8,128)(2,1)}, bf16[48,208,208]{2,1,0:T(8,128)(2,1)}, ...) custom-call(f32[2,48,288]{2,1,0:T(8,128)} %rest_0_.1, ...), custom_call_target="tpu_custom_call" | custom-call | tf_op jit(solution)/shard_map/gather_forward/pallas_call | solution.py:1055
  62.8 63.6 %second_block.1 = (bf16[1528,384]{1,0:T(8,128)(2,1)}, bf16[32,384]{1,0:T(8,128)(2,1)}, f32[1664,384]{1,0:T(8,128)}, bf16[3,2,2,4,2,48,384]{6,5,4,3,2,1,0:T(8,128)(2,1)}, f32[16,384]{1,0:T(8,128)}) custom-call(s32[1,1]{1,0:T(1,128)S(6)} %copy.40.count_ref, f32[1664,384]{1,0:T(8,128)} %get-tuple-element.66.h_ref, bf16[1664,384]{1,0:T(8,128)(2,1)} %get-tuple-element.67.cot_ref, ...), custom_call_target="tpu_custom_call" | custom-call | tf_op jit(solution)/shard_map/second_block/pallas_call | solution.py:568
  126.5 65.0 %backward_scatter.1 = (f32[1528,384]{1,0:T(8,128)}, f32[3,48,384]{2,1,0:T(8,128)}, f32[3,48,384]{2,1,0:T(8,128)}, f32[32,384]{1,0:T(8,128)}, bf16[8,32,384]{2,1,0:T(8,128)(2,1)}) custom-call(f32[1664,384]{1,0:T(8,128)} %get-tuple-element.75.dy_ref, bf16[1664,384]{1,0:T(8,128)(2,1)} %get-tuple-element.76.x_ref, bf16[1664,384]{1,0:T(8,128)(2,1)} %get-tuple-element.77.a1_hbm, ...), custom_call_target="tpu_custom_call" | custom-call | tf_op jit(solution)/shard_map/backward_scatter/pallas_call | solution.py:1320
  191.4 0.0 copy-start
  191.4 3.4 %apply_updates.1 = (f32[2,48,288]{2,1,0:T(8,128)}, f32[2,48,96]{2,1,0:T(8,128)}, f32[2,48,384]{2,1,0:T(8,128)}, f32[2,192,96]{2,1,0:T(8,128)}, f32[2,48,288]{2,1...) custom-call(f32[3,48,384]{2,1,0:T(8,128)} %get-tuple-element.93.low_, ...), custom_call_target="tpu_custom_call" | custom-call | tf_op jit(solution)/shard_map/apply_updates/pallas_call | solution.py:1410
  194.8 0.0 copy-done
  194.9 1.4 copy.41
Async XLA Ops:
  191.4 3.4 %copy-start = (f32[1528,384]{1,0:T(8,128)S(1)}, f32[1528,384]{1,0:T(8,128)}, u32[]{:S(2)}) copy-start(f32[1528,384]{1,0:T(8,128)} %get-tuple-element.98) | copy-start | bytes 7041028
